TPU v7x, 128 devices: a whole 4x4x4 slice. The times are simulated.
128 devices in a mesh: sfc: 8 (over x, core), node: 16 (over z, y).
Axes of the slice: x: 4, y: 4, z: 4, core: 2. Of those that a mesh axis runs over, the one named last changes fastest.
Arguments:
- fine_state: float32 [128, 21, 32, 1024], P(('sfc', 'node')), may hold values from -6 to 6
- conduct: float32 [128, 32, 1024], P(('sfc', 'node')), may hold values from 0.2 to 2
- spec_rate: float32 [21], replicated, may hold values from 0.1 to 1
- reaction: float32 [21, 21], replicated, may hold values from -2 to 2
- coarse_state: float32 [128, 21, 32, 1024], P(('sfc', 'node')), may hold values from -6 to 6
- ghost_source: int32 [128, 6], P(('sfc', 'node')), may hold values from -1 to 287, as said below
- parent_box: int32 [128], P(('sfc', 'node')), may hold values from 0 to 127
Outputs:
- tendency: float32 [128, 21, 32, 1024], P(('sfc', 'node'))
- register: float32 [128, 48, 21, 256], P(('sfc', 'node'))
Inputs may be any that keep to these rules, and one draw needn't show every extreme that they name: ghost_source is -1 on about a third of the faces; box 0 names the largest index on face 0 and is coarse-fine on face 1.
All inputs are finite; a program needn't handle non-finite values.
Results may differ from a plain program's by a relative error of at most 0.0003.
Values sent between devices are 32-bit elements; how exact they have to be, the bound alone decides.
No kernel may reach another device: no remote copies, remote signals or barrier semaphores. Data moves between devices by JAX's collectives and lax.ppermute only.
A program may use at most 256 MiB of HBM per device.

v0:
```python
import functools

import jax
import jax.numpy as jnp
import numpy as np
from jax import lax
from jax.experimental import pallas as pl
from jax.experimental.pallas import tpu as pltpu
from jax.sharding import PartitionSpec as P

S, B, AREA = 21, 32, 1024
PIECES = 16
HALF = 11
SLOTS = 24
ROWS = 12
FINE = 6 * ROWS
CROWS = 16
F32, BF16 = jnp.float32, jnp.bfloat16


def slot(s):
    return s if s < HALF else s + 1


def pick_fine():
    m = np.zeros((AREA, 128), np.float32)
    for b in range(32):
        m[b, b] = 1
        m[31 * 32 + b, 32 + b] = 1
        m[b * 32, 64 + b] = 1
        m[b * 32 + 31, 96 + b] = 1
    return m


def pick_coarse():
    m = np.zeros((AREA, 256), np.float32)
    for w, p in enumerate((0, 15, 16, 31)):
        for b in range(32):
            m[p * 32 + b, w * 32 + b] = 1
            m[b * 32 + p, 128 + w * 32 + b] = 1
    return m


def split_octants():
    m = np.zeros((256, 256), np.float32)
    for a in range(8):
        for o in range(2):
            for b in range(16):
                m[a * 32 + o * 16 + b, o * 128 + a * 16 + b] = 1
    return m


def average():
    m = np.zeros((512, 128), np.float32)
    for a in range(16):
        for b in range(32):
            m[a * 32 + b, (a // 2) * 16 + b // 2] = 0.25
    return m


def dot(x, m):
    hi = x.astype(BF16)
    lo = (x - hi.astype(F32)).astype(BF16)
    return jnp.dot(hi, m, preferred_element_type=F32) + jnp.dot(lo, m, preferred_element_type=F32)


def lanes(rows):
    return lax.broadcasted_iota(jnp.int32, (rows, 128), 1)


def swap_blocks(parts):
    block = lanes(parts[0].shape[0]) // 32
    out = []
    for f in range(4):
        acc = None
        for q in range(4):
            moved = parts[q] if q == f else pltpu.roll(parts[q], (32 * (q - f)) % 128, 1)
            acc = moved if acc is None else jnp.where(block == q, moved, acc)
        out.append(acc)
    return out


def pack_fine_kernel(source, parent, state, conduct, rate, pick, mean, fine, means, edge, xs, weighted, mr, nr):
    edge[HALF * 32 : HALF * 32 + 32, :] = jnp.zeros((32, 128), F32)
    edge[22 * 32 : 23 * 32, :] = jnp.zeros((32, 128), F32)
    xs[...] = jnp.zeros_like(xs)
    sel = pick[...]
    for lo, hi in ((0, 6), (6, 11), (11, 16), (16, 21)):
        got = dot(state[0, lo:hi].reshape((hi - lo) * 32, AREA), sel)
        edge[slot(lo) * 32 : (slot(lo) + hi - lo) * 32, :] = got
    edge[23 * 32 : 24 * 32, :] = dot(conduct[0], sel)
    for s in range(S):
        xs[0, slot(s) : slot(s) + 1, :] = state[0, s, 0:1, :]
        xs[1, slot(s) : slot(s) + 1, :] = state[0, s, 31:32, :]
    xs[0, 23:24, :] = conduct[0, 0:1, :]
    xs[1, 23:24, :] = conduct[0, 31:32, :]
    row = lax.broadcasted_iota(jnp.int32, (SLOTS, 128), 0)
    rates = jnp.broadcast_to(rate[...], (SLOTS, 128))
    for k in range(8):
        across = [xs[side, :, 128 * k : 128 * k + 128] for side in range(2)]
        across += swap_blocks([edge[pl.ds(4 * k + q, SLOTS, stride=32), :] for q in range(4)])
        k2, kk = k // 4, k % 4
        for f in range(6):
            t = across[f]
            fine[2 * k, f * ROWS : (f + 1) * ROWS, :] = t[:ROWS]
            fine[2 * k + 1, f * ROWS : (f + 1) * ROWS, :] = t[ROWS:]
            kap = jnp.broadcast_to(t[23:24], (SLOTS, 128))
            at = (f * 2 + k2) * SLOTS
            weighted[at : at + SLOTS, 128 * kk : 128 * kk + 128] = jnp.where(row == 23, t, t * kap * rates)
    lane = lanes(1)
    note = jnp.where(lane == 6, parent[0], 0)
    for f in range(6):
        note = jnp.where(lane == f, source[0, f], note)
    fine[:, 11:12, :] = jnp.broadcast_to(note.astype(F32)[None], (PIECES, 1, 128))
    averaged = dot(weighted[...], mean[...])
    mr[...] = jnp.zeros_like(mr)
    nr[...] = jnp.zeros_like(nr)
    for f in range(6):
        keep = jnp.where(source[0, f] < 0, 1.0, 0.0).astype(F32)
        for k2 in range(2):
            fk = f * 2 + k2
            first = averaged[fk * SLOTS : (fk + 1) * SLOTS] * keep
            second = jnp.broadcast_to(first[23:24], (SLOTS, 128)) * rates
            for ref, v in ((mr, first), (nr, second)):
                ref[fk * S : fk * S + HALF, :] = v[:HALF]
                ref[fk * S + HALF : (fk + 1) * S, :] = v[ROWS : ROWS + S - HALF]
    for j in range(PIECES):
        means[j, :CROWS, :] = mr[j * CROWS : (j + 1) * CROWS, :]
        means[j, CROWS:, :] = nr[j * CROWS : (j + 1) * CROWS, :]


def turn(x):
    n = x.shape[0] // 8
    x = x.reshape(n, 8, 128)
    row = lax.broadcasted_iota(jnp.int32, (n, 8, 128), 1)
    group = lax.broadcasted_iota(jnp.int32, (n, 8, 128), 2) // 16
    for d in (1, 2, 4):
        up = pltpu.roll(pltpu.roll(x, 8 - d, 1), 16 * d, 2)
        down = pltpu.roll(pltpu.roll(x, d, 1), 128 - 16 * d, 2)
        rb, gb = row & d, group & d
        x = jnp.where(rb == gb, x, jnp.where(rb == 0, up, down))
    return x.reshape(n * 8, 128)


def pack_coarse_kernel(coarse, means, pick, octs, out, turned, planes, table):
    sel = pick[...]
    for lo in range(0, S, 7):
        got = dot(coarse[0, lo : lo + 7].reshape(224, AREA), sel)
        turned[0, lo * 32 : (lo + 7) * 32, :] = got[:, :128]
        turned[1, lo * 32 : (lo + 7) * 32, :] = got[:, 128:]
    for t in range(2):
        for lo in range(S):
            turned[t, lo * 32 : (lo + 1) * 32, :] = turn(turned[t, lo * 32 : (lo + 1) * 32, :])
    planes[...] = jnp.zeros_like(planes)
    for w, p in enumerate((0, 15, 16, 31)):
        for s in range(S):
            planes[w * SLOTS + s : w * SLOTS + s + 1, :] = coarse[0, s, p : p + 1, :]
    for o in range(8):
        table[o, 12 * S :, :] = jnp.zeros((256 - 12 * S, 128), F32)
    for oy in range(2):
        for k2 in range(2):
            c = oy * 2 + k2
            got = dot(planes[:, 256 * c : 256 * c + 256], octs[...])
            for w in range(4):
                for oz in range(2):
                    o, fk = 4 * (w // 2) + 2 * oy + oz, (w % 2) * 2 + k2
                    table[o, fk * S : (fk + 1) * S, :] = got[w * SLOTS : w * SLOTS + S, oz * 128 : oz * 128 + 128]
    for t in range(2):
        for g in range(4):
            ox, k2 = g // 2, g % 2
            for w in range(4):
                for i in range(2):
                    oy, oz = (w // 2, i) if t == 0 else (i, w // 2)
                    f = 2 + 2 * t + w % 2
                    fk = f * 2 + k2
                    table[4 * ox + 2 * oy + oz, fk * S : (fk + 1) * S, :] = turned[
                        t, pl.ds(g * 8 + w * 2 + i, S, stride=32), :
                    ]
    for j in range(PIECES):
        for o in range(8):
            out[j, o * CROWS : (o + 1) * CROWS, :] = table[o, j * CROWS : (j + 1) * CROWS, :]
        out[j, 8 * CROWS :, :] = means[j]


def inner_kernel(rate, state, conduct, react, out, coef):
    kap = conduct[0]
    react_hi = react[...].astype(BF16)
    react_lo = (react[...] - react_hi.astype(F32)).astype(BF16)
    col = lax.broadcasted_iota(jnp.int32, (B, AREA), 1)
    row = lax.broadcasted_iota(jnp.int32, (B, AREA), 0)
    y, z = col // 32, col % 32
    diag = jnp.zeros((B, AREA), F32)
    for i, (axis, step, at, end) in enumerate(
        ((0, 1, row, 0), (0, B - 1, row, 31), (1, 32, y, 0), (1, AREA - 32, y, 31), (1, 1, z, 0), (1, AREA - 1, z, 31))
    ):
        edge = at == end
        c = 0.5 * (kap + pltpu.roll(kap, step, axis))
        diag = diag + jnp.where(edge, kap, c)
        coef[i] = jnp.where(edge, 0.0, c)
    coef[6] = diag
    for g in range(4):
        x = state[0, :, g * 8 : g * 8 + 8, :].reshape(S * 8, AREA)
        hi = x.astype(BF16)
        lo = (x - hi.astype(F32)).astype(BF16)
        got = jnp.dot(react_hi, hi, preferred_element_type=F32)
        got += jnp.dot(react_hi, lo, preferred_element_type=F32)
        got += jnp.dot(react_lo, hi, preferred_element_type=F32)
        out[0, :, g * 8 : g * 8 + 8, :] = got.reshape(S, 8, AREA)

    def species(s, carry):
        u = state[0, s]
        acc = -coef[6] * u
        for i, (axis, step) in enumerate(((0, 1), (0, B - 1), (1, 32), (1, AREA - 32), (1, 1), (1, AREA - 1))):
            acc = acc + coef[i] * pltpu.roll(u, step, axis)
        out[0, s] = out[0, s] + rate[s] * acc
        return carry

    lax.fori_loop(0, S, species, 0)


def relay_coarse_kernel(note, got, ghosts, register):
    register[...] = jnp.zeros_like(register)
    for n in range(PIECES):
        p = note[n, 6]
        c, o = p // 8, pl.multiple_of((p % 8) * CROWS, CROWS)
        piece = got[c, pl.ds(o, CROWS), :]
        ghosts[n] = piece
        flux = got[n, 8 * CROWS : 9 * CROWS, :] - got[n, 9 * CROWS :, :] * piece
        register[c, pl.ds(o, CROWS), :] = register[c, pl.ds(o, CROWS), :] + flux


def relay_fine_kernel(note, before, own, after, ghosts, out, table):
    for g, ref in enumerate((before, own, after)):
        for n in range(PIECES):
            for f in range(6):
                table[g * 96 + n * 6 + f, :ROWS, :] = ref[n, f * ROWS : (f + 1) * ROWS, :]
    for n in range(PIECES):
        for f in range(6):
            q = jnp.maximum(note[n, f], 0)
            out[n, f * ROWS : (f + 1) * ROWS, :] = table[q, :ROWS, :]
        out[n, FINE:, :] = ghosts[n]


def outer_kernel(rate, source, inner, got, conduct, spread, place, out, crow, cslot, wide, xs, edge):
    for j in range(PIECES):
        crow[j * CROWS : (j + 1) * CROWS, :] = got[j, FINE:, :]
    cslot[...] = jnp.zeros_like(cslot)
    for fk in range(12):
        cslot[fk * SLOTS : fk * SLOTS + HALF, :] = crow[fk * S : fk * S + HALF, :]
        cslot[fk * SLOTS + ROWS : fk * SLOTS + ROWS + S - HALF, :] = crow[fk * S + HALF : (fk + 1) * S, :]
    wide[...] = dot(cslot[...], spread[...])
    for k in range(8):
        k2, kk = k // 4, k % 4
        slabs = []
        for f in range(6):
            fine = jnp.concatenate(
                [got[2 * k, f * ROWS : (f + 1) * ROWS, :], got[2 * k + 1, f * ROWS : (f + 1) * ROWS, :]], 0
            )
            at = (f * 2 + k2) * SLOTS
            slabs.append(jnp.where(source[0, f] >= 0, fine, wide[at : at + SLOTS, 128 * kk : 128 * kk + 128]))
        for side in range(2):
            xs[side, :, 128 * k : 128 * k + 128] = slabs[side]
        for q, v in enumerate(swap_blocks(slabs[2:])):
            edge[pl.ds(4 * k + q, SLOTS, stride=32), :] = v
    kap = conduct[0]
    row = lax.broadcasted_iota(jnp.int32, (B, AREA), 0)
    for lo, hi in ((0, 6), (6, 11), (11, 16), (16, 21)):
        ghost = dot(edge[slot(lo) * 32 : (slot(lo) + hi - lo) * 32, :], place[...])
        for s in range(lo, hi):
            mine = ghost[(s - lo) * 32 : (s - lo + 1) * 32]
            mine = mine + jnp.where(row == 0, xs[0, slot(s) : slot(s) + 1, :], 0.0)
            mine = mine + jnp.where(row == 31, xs[1, slot(s) : slot(s) + 1, :], 0.0)
            out[0, s] = inner[0, s] + rate[s] * (kap * mine)


def unpack_register_kernel(got, out, table):
    for j in range(PIECES):
        for o in range(8):
            table[o, j * CROWS : (j + 1) * CROWS, :] = got[j, o * CROWS : (o + 1) * CROWS, :]
    for o in range(8):
        for f in range(6):
            for k2 in range(2):
                fk = f * 2 + k2
                out[0, o * 6 + f, :, k2 * 128 : k2 * 128 + 128] = table[o, fk * S : (fk + 1) * S, :]


VM = pl.BlockSpec(memory_space=pltpu.VMEM)
SM = pl.BlockSpec(memory_space=pltpu.SMEM)


def call(kernel, ins, outs, scratch, args, flops=0, limit=40):
    many = isinstance(outs, list)
    shapes = [jax.ShapeDtypeStruct(o, F32) for o in (outs if many else [outs])]
    moved = sum(a.size * a.dtype.itemsize for a in args) + sum(4 * int(np.prod(o.shape)) for o in shapes)
    return pl.pallas_call(
        kernel,
        out_shape=shapes if many else shapes[0],
        in_specs=[SM if c == "s" else VM for c in ins],
        out_specs=[VM] * len(shapes) if many else VM,
        scratch_shapes=[pltpu.VMEM(s, F32) for s in scratch],
        compiler_params=pltpu.CompilerParams(vmem_limit_bytes=limit << 20),
        cost_estimate=pl.CostEstimate(flops=flops, bytes_accessed=moved, transcendentals=0),
        name=kernel.__name__.removesuffix("_kernel"),
    )(*args)


def shifted(block, distance):
    devices = range(lax.axis_size("sfc"))
    return lax.ppermute(block, "sfc", [(i, i + distance) for i in devices if i + distance in devices])


def exchange(block):
    return lax.all_to_all(block, "node", 0, 0, tiled=True)


def local(fine_state, conduct, spec_rate, reaction, coarse_state, ghost_source, parent_box):
    zero = jnp.zeros((1,), F32)
    rates = jnp.concatenate([spec_rate[:HALF], zero, spec_rate[HALF:], zero, zero])[:, None]
    pick = jnp.asarray(pick_fine(), BF16)
    place = jnp.asarray(pick_fine().T, BF16)
    mean = jnp.asarray(average(), BF16)
    spread = jnp.asarray(4 * average().T, BF16)
    fine, means = call(
        pack_fine_kernel,
        "ssvvvvv",
        [(PIECES, FINE, 128), (PIECES, 2 * CROWS, 128)],
        [(SLOTS * 32, 128), (2, SLOTS, AREA), (12 * SLOTS, 512), (256, 128), (256, 128)],
        (ghost_source, parent_box, fine_state, conduct, rates, pick, mean),
        int(1e9),
    )
    own = exchange(fine)
    coarse = call(
        pack_coarse_kernel,
        "vvvv",
        (PIECES, 10 * CROWS, 128),
        [(2, S * 32, 128), (4 * SLOTS, AREA), (8, 256, 128)],
        (coarse_state, means, jnp.asarray(pick_coarse(), BF16), jnp.asarray(split_octants(), BF16)),
        int(1e9),
    )
    grouped = exchange(coarse)
    before, after = shifted(own, 1), shifted(own, -1)
    react = jnp.kron(reaction, jnp.eye(8, dtype=F32))
    inner = call(
        inner_kernel,
        "svvv",
        (1, S, B, AREA),
        [(7, B, AREA)],
        (spec_rate, fine_state, conduct, react),
        int(1e9),
    )
    note = own[:, 11, :8].astype(jnp.int32)
    ghosts, rows = call(
        relay_coarse_kernel,
        "sv",
        [(PIECES, CROWS, 128), (PIECES, 8 * CROWS, 128)],
        [],
        (note, grouped),
    )
    chosen = call(
        relay_fine_kernel,
        "svvvv",
        (PIECES, FINE + CROWS, 128),
        [(3 * 96, ROWS, 128)],
        (note, before, own, after, ghosts),
    )
    mine = exchange(chosen)
    rows = exchange(rows)
    tendency = call(
        outer_kernel,
        "ssvvvvv",
        (1, S, B, AREA),
        [(256, 128), (12 * SLOTS, 128), (12 * SLOTS, 512), (2, SLOTS, AREA), (SLOTS * 32, 128)],
        (spec_rate, ghost_source, inner, mine, conduct, spread, place),
        int(1e9),
    )
    register = call(unpack_register_kernel, "v", (1, 48, S, 256), [(8, 256, 128)], (rows,))
    return tendency, register


def solution(mesh):
    box = P(("sfc", "node"))
    return jax.shard_map(
        local,
        mesh=mesh,
        in_specs=(box, box, P(), P(), box, box, box),
        out_specs=(box, box),
        check_vma=False,
    )
```

profile of v0, /device:TPU:0, one launch (start us, length us, event | category | flops | bytes accessed | tf_op | source)
XLA Modules:
  0.0 94.7 jit_solution(4943855649628537827)
XLA Ops:
  1.3 0.7 slice.10
  2.0 0.7 maximum_bitcast_fusion
  2.7 0.1 copy.25.rate
  2.8 1.8 %copy-done.1 = f32[1,21,32,1024]{3,2,1,0:T(8,128)S(1)} copy-done((f32[1,21,32,1024]{3,2,1,0:T(8,128)S(1)}, f32[1,21,32,1024]{3,2,1,0:T(8,128)}, u32[]{:S(2)}) %copy-start.1) | copy-done | bytes 2752536
  4.6 0.9 copy-done.5
  5.5 0.7 copy-done.13
  6.2 0.9 %copy-done.15 = bf16[1024,128]{1,0:T(8,128)(2,1)S(1)} copy-done((bf16[1024,128]{1,0:T(8,128)(2,1)S(1)}, bf16[1024,128]{1,0:T(8,128)(2,1)}, u32[]{:S(2)}) %copy-start.15) | copy-done | bytes 262168
  7.1 0.9 copy-done.16
  8.0 2.1 %pack_fine.1 = (f32[16,72,128]{2,1,0:T(8,128)S(1)}, f32[16,32,128]{2,1,0:T(8,128)S(1)}) custom-call(s32[1,6]{1,0:T(1,128)S(1)} %copy-done.13, s32[1]{0:T(128)S(6)} %copy.31.parent, f32[1,21,32,1024]{3,2,1,0:T(8,128)S(1)} %copy-done.1, f32[1,32,1024]{2,1,0:T(8,128)S(1)} %copy-done.5, f32[24,1]{1,0:T(8,128)S(1)} %copy.25.rate, ...), custom_call_target="tpu_custom_call" | custom-call | flops 1000000000 | bytes 4128892 | tf_op jit(solution)/shard_map/pack_fine/pallas_call | solution.py:295
  10.1 0.0 copy-start.3
  10.1 0.8 copy-done.3
  10.9 0.7 copy-done.8
  11.6 8.1 %all-to-all-start = ((f32[16,72,128]{2,1,0:T(8,128)}), f32[16,72,128]{2,1,0:T(8,128)S(1)}, u32[]{:S(2)}, u32[]{:S(2)}) async-start(f32[16,72,128]{2,1,0:T(8,128)} %copy-done.3), calls=%async_computation | async-start | bytes 1179648 | tf_op jit(solution)/shard_map/all_to_all | solution.py:313
  19.8 0.0 copy-done
  19.8 0.0 copy-done.11
  19.8 0.0 copy-start.4
  19.8 1.0 %copy-done.4 = bf16[1024,256]{1,0:T(8,128)(2,1)S(1)} copy-done((bf16[1024,256]{1,0:T(8,128)(2,1)S(1)}, bf16[1024,256]{1,0:T(8,128)(2,1)}, u32[]{:S(2)}) %copy-start.4) | copy-done | bytes 524312
  20.8 0.9 %copy-done.9 = f32[16,32,128]{2,1,0:T(8,128)S(1)} copy-done((f32[16,32,128]{2,1,0:T(8,128)S(1)}, f32[16,32,128]{2,1,0:T(8,128)}, u32[]{:S(2)}) %copy-start.9) | copy-done | bytes 262168
  21.8 3.1 %pack_coarse.1 = f32[16,160,128]{2,1,0:T(8,128)} custom-call(f32[1,21,32,1024]{3,2,1,0:T(8,128)S(1)} %copy-done, f32[16,32,128]{2,1,0:T(8,128)S(1)} %copy-done.9, bf16[1024,256]{1,0:T(8,128)(2,1)S(1)} %copy-done.4, bf16[256,256]{1,0:T(8,128)(2,1)S(1)} %copy-done.11), custom_call_target="tpu_custom_call" | custom-call | flops 1000000000 | bytes 4980736 | tf_op jit(solution)/shard_map/pack_coarse/pallas_call | solution.py:295
  24.9 7.1 %all-to-all-done.own = f32[16,72,128]{2,1,0:T(8,128)S(1)} async-done(((f32[16,72,128]{2,1,0:T(8,128)}), f32[16,72,128]{2,1,0:T(8,128)S(1)}, u32[]{:S(2)}, u32[]{:S(2)}) %all-to-all-start) | async-done | bytes 589856 | tf_op jit(solution)/shard_map/all_to_all | solution.py:313
  32.0 3.7 %all-to-all-start.1 = ((f32[16,160,128]{2,1,0:T(8,128)}), f32[16,160,128]{2,1,0:T(8,128)S(1)}, u32[]{:S(2)}, u32[]{:S(2)}) async-start(f32[16,160,128]{2,1,0:T(8,128)} %pack_coarse.1), calls=%async_computation.1 | async-start | bytes 2621440 | tf_op jit(solution)/shard_map/all_to_all | solution.py:313
  35.7 1.3 %collective-permute-start.1 = (f32[16,72,128]{2,1,0:T(8,128)S(1)}, f32[16,72,128]{2,1,0:T(8,128)S(1)}, u32[]{:S(2)}, u32[]{:S(2)}) collective-permute-start(f32[16,72,128]{2,1,0:T(8,128)S(1)} %all-to-all-done.own), channel_id=1, source_target_pairs={{16,0},{32,16},{48,32},{64,48},{80,64},{96,80},{112,96},{17,1},{33... | collective-permute-start | bytes 1769480 | tf_op jit(solution)/shard_map/ppermute | solution.py:309
  37.0 3.1 %collective-permute-start = (f32[16,72,128]{2,1,0:T(8,128)S(1)}, f32[16,72,128]{2,1,0:T(8,128)S(1)}, u32[]{:S(2)}, u32[]{:S(2)}) collective-permute-start(f32[16,72,128]{2,1,0:T(8,128)S(1)} %all-to-all-done.own), channel_id=1, source_target_pairs={{0,16},{16,32},{32,48},{48,64},{64,80},{80,96},{96,112},{1,17},{17... | collective-permute-start | bytes 1769480 | tf_op jit(solution)/shard_map/ppermute | solution.py:309
  40.1 14.9 %all-to-all-done.1.got = f32[16,160,128]{2,1,0:T(8,128)S(1)} async-done(((f32[16,160,128]{2,1,0:T(8,128)}), f32[16,160,128]{2,1,0:T(8,128)S(1)}, u32[]{:S(2)}, u32[]{:S(2)}) %all-to-all-start.1) | async-done | bytes 1310752 | tf_op jit(solution)/shard_map/all_to_all | solution.py:313
  55.0 1.8 %relay_coarse.1 = (f32[16,16,128]{2,1,0:T(8,128)S(1)}, f32[16,128,128]{2,1,0:T(8,128)}) custom-call(s32[16,8]{1,0:T(8,128)S(1)} %bitcast.4, f32[16,160,128]{2,1,0:T(8,128)S(1)} %all-to-all-done.1.got), custom_call_target="tpu_custom_call" | custom-call | bytes 2490880 | tf_op jit(solution)/shard_map/relay_coarse/pallas_call | solution.py:295
  56.9 0.0 collective-permute-done.1.after
  56.9 0.0 collective-permute-done.before
  56.9 1.0 %relay_fine.1 = f32[16,88,128]{2,1,0:T(8,128)S(1)} custom-call(s32[16,8]{1,0:T(8,128)S(1)} %bitcast.5, f32[16,72,128]{2,1,0:T(8,128)S(1)} %collective-permute-done.before, f32[16,72,128]{2,1,0:T(8,128)S(1)} %all-to-all-done.own, f32[16,72,128]{2,1,0:T(8,128)S(1)} %collective-permute-done.1.after, f32[16,16,128]{2,1,0:T(8,128)S(1)} %get-tuple-element.8.ghosts), custom_call_target="tpu_custom_call" | custom-call | bytes 2621952 | tf_op jit(solution)/shard_map/relay_fine/pallas_call | solution.py:295
  57.8 0.0 copy-start.17
  57.8 15.8 %all_to_all.20.got = f32[16,88,128]{2,1,0:T(8,128)S(1)} all-to-all(f32[16,88,128]{2,1,0:T(8,128)S(1)} %relay_fine.1), channel_id=1, replica_groups=mesh['sfc'=8,'node'=16] {'node'}, dimensions={0} | all-to-all | bytes 1441792 | tf_op jit(solution)/shard_map/all_to_all | solution.py:313
  73.7 3.7 %all-to-all-start.3 = ((f32[16,128,128]{2,1,0:T(8,128)}), f32[16,128,128]{2,1,0:T(8,128)S(1)}, u32[]{:S(2)}, u32[]{:S(2)}) async-start(f32[16,128,128]{2,1,0:T(8,128)} %get-tuple-element.9), calls=%async_computation.3 | async-start | bytes 2097152 | tf_op jit(solution)/shard_map/all_to_all | solution.py:313
  77.3 0.0 copy-done.17
  77.3 0.0 copy-start.6
  77.4 0.0 copy-start.12
  77.4 1.5 %broadcast_multiply_fusion = f32[21,8,21,8]{3,2,1,0:T(8,128)} fusion(f32[8,8]{1,0:T(8,128)S(1)} %fusion, f32[21,21]{1,0:T(8,128)S(1)} %copy-done.17), kind=kLoop, calls=%fused_computation | loop fusion | flops 28224 | bytes 114916 | tf_op jit(solution)/shard_map/jit(kron)/mul | solution.py:342
  78.9 2.2 %mul.27.react = f32[168,168]{1,0:T(8,128)S(1)} reshape(f32[21,8,21,8]{3,2,1,0:T(8,128)} %broadcast_multiply_fusion) | data formatting | bytes 225792 | tf_op jit(solution)/shard_map/jit(kron)/mul | solution.py:342
  81.1 0.0 copy-done.6
  81.1 0.0 copy-done.12
  81.1 0.0 copy-start.2
  81.1 1.8 %copy-done.2 = f32[1,21,32,1024]{3,2,1,0:T(8,128)S(1)} copy-done((f32[1,21,32,1024]{3,2,1,0:T(8,128)S(1)}, f32[1,21,32,1024]{3,2,1,0:T(8,128)}, u32[]{:S(2)}) %copy-start.2) | copy-done | bytes 2752536
  82.9 6.3 %inner.1 = f32[1,21,32,1024]{3,2,1,0:T(8,128)S(1)} custom-call(f32[21]{0:T(128)S(1)} %copy-done.12, f32[1,21,32,1024]{3,2,1,0:T(8,128)S(1)} %copy-done.2, f32[1,32,1024]{2,1,0:T(8,128)S(1)} %copy-done.6, f32[168,168]{1,0:T(8,128)S(1)} %mul.27.react), custom_call_target="tpu_custom_call" | custom-call | flops 1000000000 | bytes 5749076 | tf_op jit(solution)/shard_map/inner/pallas_call | solution.py:295
  89.2 0.0 copy-done.7
  89.2 0.0 copy-done.10
  89.2 0.0 copy-done.14
  89.2 3.5 %outer.1 = f32[1,21,32,1024]{3,2,1,0:T(8,128)} custom-call(f32[21]{0:T(128)S(1)} %copy-done.12, s32[1,6]{1,0:T(1,128)S(1)} %copy-done.14, f32[1,21,32,1024]{3,2,1,0:T(8,128)S(1)} %inner.1, f32[16,88,128]{2,1,0:T(8,128)S(1)} %all_to_all.20.got, f32[1,32,1024]{2,1,0:T(8,128)S(1)} %copy-done.6, bf16[128,512]{1,0:T(8,128)(2,1)S(1)} %copy-done.10, ...), custom_call_target="tpu_custom_call" | custom-call | flops 1000000000 | bytes 6750316 | tf_op jit(solution)/shard_map/outer/pallas_call | solution.py:295
  92.7 0.5 all-to-all-done.3.got
  93.3 0.1 unpack_register.1
  93.4 1.3 %copy.29 = f32[1,48,21,256]{3,1,2,0:T(8,128)} copy(f32[1,48,21,256]{3,2,1,0:T(8,128)S(1)} %unpack_register.1) | data formatting | bytes 2064384
  (15 shorter events, 0.0 us)
Async XLA Ops:
  2.8 1.8 %copy-start.1 = (f32[1,21,32,1024]{3,2,1,0:T(8,128)S(1)}, f32[1,21,32,1024]{3,2,1,0:T(8,128)}, u32[]{:S(2)}) copy-start(f32[1,21,32,1024]{3,2,1,0:T(8,128)} %state.3) | copy-start | bytes 8257540
  4.6 0.9 copy-start.5
  5.5 0.7 copy-start.13
  6.2 0.9 %copy-start.15 = (bf16[1024,128]{1,0:T(8,128)(2,1)S(1)}, bf16[1024,128]{1,0:T(8,128)(2,1)}, u32[]{:S(2)}) copy-start(bf16[1024,128]{1,0:T(8,128)(2,1)} %constant.16.clone.pick) | copy-start | bytes 786436
  7.1 0.9 copy-start.16
  8.0 11.8 %copy-start = (f32[1,21,32,1024]{3,2,1,0:T(8,128)S(1)}, f32[1,21,32,1024]{3,2,1,0:T(8,128)}, u32[]{:S(2)}) copy-start(f32[1,21,32,1024]{3,2,1,0:T(8,128)} %coarse.1) | copy-start | bytes 8257540
  8.0 11.8 %copy-start.11 = (bf16[256,256]{1,0:T(8,128)(2,1)S(1)}, bf16[256,256]{1,0:T(8,128)(2,1)}, u32[]{:S(2)}) copy-start(bf16[256,256]{1,0:T(8,128)(2,1)} %constant.21.clone.octs) | copy-start | bytes 393220
  10.1 0.8 copy-start.3
  10.9 0.7 copy-start.8
  11.6 20.4 %all-to-all-start = ((f32[16,72,128]{2,1,0:T(8,128)}), f32[16,72,128]{2,1,0:T(8,128)S(1)}, u32[]{:S(2)}, u32[]{:S(2)}) async-start(f32[16,72,128]{2,1,0:T(8,128)} %copy-done.3), calls=%async_computation | async-start | bytes 1179648 | tf_op jit(solution)/shard_map/all_to_all | solution.py:313
  19.8 1.0 %copy-start.4 = (bf16[1024,256]{1,0:T(8,128)(2,1)S(1)}, bf16[1024,256]{1,0:T(8,128)(2,1)}, u32[]{:S(2)}) copy-start(bf16[1024,256]{1,0:T(8,128)(2,1)} %constant.20.clone.pick) | copy-start | bytes 1572868
  20.8 0.9 %copy-start.9 = (f32[16,32,128]{2,1,0:T(8,128)S(1)}, f32[16,32,128]{2,1,0:T(8,128)}, u32[]{:S(2)}) copy-start(f32[16,32,128]{2,1,0:T(8,128)} %copy-done.8) | copy-start | bytes 786436
  32.0 23.0 %all-to-all-start.1 = ((f32[16,160,128]{2,1,0:T(8,128)}), f32[16,160,128]{2,1,0:T(8,128)S(1)}, u32[]{:S(2)}, u32[]{:S(2)}) async-start(f32[16,160,128]{2,1,0:T(8,128)} %pack_coarse.1), calls=%async_computation.1 | async-start | bytes 2621440 | tf_op jit(solution)/shard_map/all_to_all | solution.py:313
  35.7 21.1 %collective-permute-start.1 = (f32[16,72,128]{2,1,0:T(8,128)S(1)}, f32[16,72,128]{2,1,0:T(8,128)S(1)}, u32[]{:S(2)}, u32[]{:S(2)}) collective-permute-start(f32[16,72,128]{2,1,0:T(8,128)S(1)} %all-to-all-done.own), channel_id=1, source_target_pairs={{16,0},{32,16},{48,32},{64,48},{80,64},{96,80},{112,96},{17,1},{33... | collective-permute-start | bytes 1769480 | tf_op jit(solution)/shard_map/ppermute | solution.py:309
  37.0 19.8 %collective-permute-start = (f32[16,72,128]{2,1,0:T(8,128)S(1)}, f32[16,72,128]{2,1,0:T(8,128)S(1)}, u32[]{:S(2)}, u32[]{:S(2)}) collective-permute-start(f32[16,72,128]{2,1,0:T(8,128)S(1)} %all-to-all-done.own), channel_id=1, source_target_pairs={{0,16},{16,32},{32,48},{48,64},{64,80},{80,96},{96,112},{1,17},{17... | collective-permute-start | bytes 1769480 | tf_op jit(solution)/shard_map/ppermute | solution.py:309
  57.8 19.5 %copy-start.17 = (f32[21,21]{1,0:T(8,128)S(1)}, f32[21,21]{1,0:T(8,128)}, u32[]{:S(2)}) copy-start(f32[21,21]{1,0:T(8,128)} %param.16) | copy-start | bytes 5296
  73.7 19.6 %all-to-all-start.3 = ((f32[16,128,128]{2,1,0:T(8,128)}), f32[16,128,128]{2,1,0:T(8,128)S(1)}, u32[]{:S(2)}, u32[]{:S(2)}) async-start(f32[16,128,128]{2,1,0:T(8,128)} %get-tuple-element.9), calls=%async_computation.3 | async-start | bytes 2097152 | tf_op jit(solution)/shard_map/all_to_all | solution.py:313
  77.3 3.7 %copy-start.6 = (f32[1,32,1024]{2,1,0:T(8,128)S(1)}, f32[1,32,1024]{2,1,0:T(8,128)}, u32[]{:S(2)}) copy-start(f32[1,32,1024]{2,1,0:T(8,128)} %conduct.5) | copy-start | bytes 393220
  77.4 3.7 %copy-start.12 = (f32[21]{0:T(128)S(1)}, f32[21]{0:T(128)}, u32[]{:S(2)}) copy-start(f32[21]{0:T(128)} %rate.3) | copy-start | bytes 256
  81.1 1.8 %copy-start.2 = (f32[1,21,32,1024]{3,2,1,0:T(8,128)S(1)}, f32[1,21,32,1024]{3,2,1,0:T(8,128)}, u32[]{:S(2)}) copy-start(f32[1,21,32,1024]{3,2,1,0:T(8,128)} %state.3) | copy-start | bytes 8257540
  82.9 6.3 %copy-start.7 = (bf16[128,1024]{1,0:T(8,128)(2,1)S(1)}, bf16[128,1024]{1,0:T(8,128)(2,1)}, u32[]{:S(2)}) copy-start(bf16[128,1024]{1,0:T(8,128)(2,1)} %constant.17.clone.place) | copy-start | bytes 786436
  82.9 6.3 %copy-start.10 = (bf16[128,512]{1,0:T(8,128)(2,1)S(1)}, bf16[128,512]{1,0:T(8,128)(2,1)}, u32[]{:S(2)}) copy-start(bf16[128,512]{1,0:T(8,128)(2,1)} %constant.19.clone.spread) | copy-start | bytes 393220
  82.9 6.3 %copy-start.14 = (s32[1,6]{1,0:T(1,128)S(1)}, s32[1,6]{1,0:T(1,128)}, u32[]{:S(2)}) copy-start(s32[1,6]{1,0:T(1,128)} %source.3) | copy-start | bytes 76
where the time goes:
time: 95.4 us; the launch traced here: 94.7 us
  waiting for transfers between devices  22.5 us (24%)
  starting transfers between devices  19.9 us (21%)
  Pallas kernels  18 us (19%)
  blocking collectives  15.8 us (17%)
  local copies, waits for them, and re-layouts  14.8 us (16%)
  other arithmetic  2.26 us (2%)
  between operations  1.49 us (2%)
    all_to_all x3, waiting for transfers between devices, exchange(): return lax.all_to_all(block, 'node', 0, 0, tiled=True)  22.5 us
    pallas_call x7, Pallas kernels, call(): pl.pallas_call(kernel, out_shape=shapes if many else shapes[0], in_specs=...  18 us
    all_to_all x1, blocking collectives, exchange(): return lax.all_to_all(block, 'node', 0, 0, tiled=True)  15.8 us
    all_to_all x3, starting transfers between devices, exchange(): return lax.all_to_all(block, 'node', 0, 0, tiled=True)  15.5 us
    unnamed x37, local copies, waits for them, and re-layouts  11.8 us
    ppermute x2, starting transfers between devices, shifted(): lax.ppermute(block, 'sfc', [(i, i + distance) for i in devices if i + dis...  4.36 us
    mul x1, local copies, waits for them, and re-layouts, local(): react = jnp.kron(reaction, jnp.eye(8, dtype=F32))  2.18 us
  transfers between devices with their start and end apart: 5, of which 3 were waited for; matrix products, arithmetic and copies ran while one was open for 4% of the time, Pallas kernels for 16%

commit v1 on v0

v1 whole, which is shorter than its diff:
```python
import functools

import jax
import jax.numpy as jnp
import numpy as np
from jax import lax
from jax.experimental import pallas as pl
from jax.experimental.pallas import tpu as pltpu
from jax.sharding import PartitionSpec as P

S, B, AREA = 21, 32, 1024
PIECES = 16
HALF = 11
SLOTS = 24
ROWS = 12
FINE = 6 * ROWS
CROWS = 16
F32, BF16 = jnp.float32, jnp.bfloat16


def slot(s):
    return s if s < HALF else s + 1


def pick_fine():
    m = np.zeros((AREA, 128), np.float32)
    for b in range(32):
        m[b, b] = 1
        m[31 * 32 + b, 32 + b] = 1
        m[b * 32, 64 + b] = 1
        m[b * 32 + 31, 96 + b] = 1
    return m


def pick_coarse():
    m = np.zeros((AREA, 256), np.float32)
    for w, p in enumerate((0, 15, 16, 31)):
        for b in range(32):
            m[p * 32 + b, w * 32 + b] = 1
            m[b * 32 + p, 128 + w * 32 + b] = 1
    return m


def split_octants():
    m = np.zeros((256, 256), np.float32)
    for a in range(8):
        for o in range(2):
            for b in range(16):
                m[a * 32 + o * 16 + b, o * 128 + a * 16 + b] = 1
    return m


def average():
    m = np.zeros((512, 128), np.float32)
    for a in range(16):
        for b in range(32):
            m[a * 32 + b, (a // 2) * 16 + b // 2] = 0.25
    return m


def dot(x, m):
    hi = x.astype(BF16)
    lo = (x - hi.astype(F32)).astype(BF16)
    return jnp.dot(hi, m, preferred_element_type=F32) + jnp.dot(lo, m, preferred_element_type=F32)


def lanes(rows):
    return lax.broadcasted_iota(jnp.int32, (rows, 128), 1)


def swap_blocks(parts):
    block = lanes(parts[0].shape[0]) // 32
    out = []
    for f in range(4):
        acc = None
        for q in range(4):
            moved = parts[q] if q == f else pltpu.roll(parts[q], (32 * (q - f)) % 128, 1)
            acc = moved if acc is None else jnp.where(block == q, moved, acc)
        out.append(acc)
    return out


CHUNKS = ((0, 6), (6, 11), (11, 16), (16, 21))


def begin(sems, pairs):
    copies = [pltpu.make_async_copy(src, dst, sems.at[i]) for i, (src, dst) in enumerate(pairs)]
    for c in copies:
        c.start()
    return copies


def pack_fine_kernel(
    source_in, parent_in, state_in, conduct_in, pick_in, mean_in, fine_out, weighted_out,
    source, parent, state, conduct, pick, mean, fine, weighted, edge, xs, kapw, sems,
):
    copies = begin(
        sems,
        [(pick_in, pick), (conduct_in, conduct), (state_in.at[:, 0:6], state.at[:, 0:6])]
        + [(state_in.at[:, lo:hi], state.at[:, lo:hi]) for lo, hi in CHUNKS[1:]]
        + [(mean_in, mean), (source_in, source), (parent_in, parent)],
    )
    edge[HALF * 32 : HALF * 32 + 32, :] = jnp.zeros((32, 128), F32)
    edge[22 * 32 : 23 * 32, :] = jnp.zeros((32, 128), F32)
    for side in range(2):
        for r in (11, 22):
            xs[side, r : r + 1, :] = jnp.zeros((1, AREA), F32)
    kapw[...] = jnp.zeros_like(kapw)
    copies[0].wait()
    copies[1].wait()
    sel = pick[...]
    edge[23 * 32 : 24 * 32, :] = dot(conduct[0], sel)
    xs[0, 23:24, :] = conduct[0, 0:1, :]
    xs[1, 23:24, :] = conduct[0, 31:32, :]
    for i, (lo, hi) in enumerate(CHUNKS):
        copies[2 + i].wait()
        got = dot(state[0, lo:hi].reshape((hi - lo) * 32, AREA), sel)
        edge[slot(lo) * 32 : (slot(lo) + hi - lo) * 32, :] = got
        for s in range(lo, hi):
            xs[0, slot(s) : slot(s) + 1, :] = state[0, s, 0:1, :]
            xs[1, slot(s) : slot(s) + 1, :] = state[0, s, 31:32, :]
    row = lax.broadcasted_iota(jnp.int32, (SLOTS, 128), 0)
    for k in range(8):
        across = [xs[side, :, 128 * k : 128 * k + 128] for side in range(2)]
        across += swap_blocks([edge[pl.ds(4 * k + q, SLOTS, stride=32), :] for q in range(4)])
        k2, kk = k // 4, k % 4
        for f in range(6):
            t = across[f]
            fine[2 * k, f * ROWS : (f + 1) * ROWS, :] = t[:ROWS]
            fine[2 * k + 1, f * ROWS : (f + 1) * ROWS, :] = t[ROWS:]
            at = f * 2 + k2
            kapw[at : at + 1, 128 * kk : 128 * kk + 128] = t[23:24]
            kap = jnp.broadcast_to(t[23:24], (SLOTS, 128))
            weighted[at * SLOTS : (at + 1) * SLOTS, 128 * kk : 128 * kk + 128] = t * kap
    saved = pltpu.make_async_copy(weighted, weighted_out, sems.at[9])
    saved.start()
    for c in copies[6:]:
        c.wait()
    lane = lanes(1)
    note = jnp.where(lane == 6, parent[0], 0)
    for f in range(6):
        note = jnp.where(lane == f, source[0, f], note)
    note = note.astype(F32)
    kmean = dot(kapw[...], mean[...])
    for j in range(PIECES):
        fk = CROWS * j // S
        fk2 = min((CROWS * j + CROWS - 1) // S, 11)
        fine[j, 11:12, :] = note
        fine[j, 23:24, :] = kmean[fk : fk + 1] * jnp.where(source[0, fk // 2] < 0, 1.0, 0.0)
        fine[j, 35:36, :] = kmean[fk2 : fk2 + 1] * jnp.where(source[0, fk2 // 2] < 0, 1.0, 0.0)
    sent = pltpu.make_async_copy(fine, fine_out, sems.at[10])
    sent.start()
    saved.wait()
    sent.wait()


def turn(x):
    n = x.shape[0] // 8
    x = x.reshape(n, 8, 128)
    row = lax.broadcasted_iota(jnp.int32, (n, 8, 128), 1)
    group = lax.broadcasted_iota(jnp.int32, (n, 8, 128), 2) // 16
    for d in (1, 2, 4):
        up = pltpu.roll(pltpu.roll(x, 8 - d, 1), 16 * d, 2)
        down = pltpu.roll(pltpu.roll(x, d, 1), 128 - 16 * d, 2)
        rb, gb = row & d, group & d
        x = jnp.where(rb == gb, x, jnp.where(rb == 0, up, down))
    return x.reshape(n * 8, 128)


def pack_coarse_kernel(
    rate_in, source_in, coarse_in, weighted_in, pick_in, octs_in, mean_in, out_hbm,
    rate, source, coarse, weighted, pick, octs, mean, out, turned, planes, table, mr, sems,
):
    copies = begin(
        sems,
        [(pick_in, pick)]
        + [(coarse_in.at[:, lo : lo + 7], coarse.at[:, lo : lo + 7]) for lo in range(0, S, 7)]
        + [(octs_in, octs), (mean_in, mean), (weighted_in, weighted), (rate_in, rate), (source_in, source)],
    )
    copies[0].wait()
    sel = pick[...]
    for i, lo in enumerate(range(0, S, 7)):
        copies[1 + i].wait()
        got = dot(coarse[0, lo : lo + 7].reshape(224, AREA), sel)
        for t in range(2):
            for s in range(7):
                turned[t, (lo + s) * 32 : (lo + s + 1) * 32, :] = turn(got[s * 32 : s * 32 + 32, 128 * t : 128 * t + 128])
    for c in copies[4:]:
        c.wait()
    planes[...] = jnp.zeros_like(planes)
    for w, p in enumerate((0, 15, 16, 31)):
        for s in range(S):
            planes[w * SLOTS + s : w * SLOTS + s + 1, :] = coarse[0, s, p : p + 1, :]
    for o in range(8):
        table[o, 12 * S :, :] = jnp.zeros((256 - 12 * S, 128), F32)
    for oy in range(2):
        for k2 in range(2):
            c = oy * 2 + k2
            got = dot(planes[:, 256 * c : 256 * c + 256], octs[...])
            for w in range(4):
                for oz in range(2):
                    o, fk = 4 * (w // 2) + 2 * oy + oz, (w % 2) * 2 + k2
                    table[o, fk * S : (fk + 1) * S, :] = got[w * SLOTS : w * SLOTS + S, oz * 128 : oz * 128 + 128]
    for t in range(2):
        for g in range(4):
            ox, k2 = g // 2, g % 2
            for w in range(4):
                for i in range(2):
                    oy, oz = (w // 2, i) if t == 0 else (i, w // 2)
                    f = 2 + 2 * t + w % 2
                    fk = f * 2 + k2
                    table[4 * ox + 2 * oy + oz, fk * S : (fk + 1) * S, :] = turned[
                        t, pl.ds(g * 8 + w * 2 + i, S, stride=32), :
                    ]
    row = lax.broadcasted_iota(jnp.int32, (SLOTS, 128), 0)
    rates = jnp.zeros((SLOTS, 128), F32)
    for s in range(S):
        rates = jnp.where(row == slot(s), rate[s], rates)
    averaged = dot(weighted[...], mean[...])
    mr[12 * S :, :] = jnp.zeros((256 - 12 * S, 128), F32)
    for fk in range(12):
        v = averaged[fk * SLOTS : (fk + 1) * SLOTS] * (rates * jnp.where(source[0, fk // 2] < 0, 1.0, 0.0))
        mr[fk * S : fk * S + HALF, :] = v[:HALF]
        mr[fk * S + HALF : (fk + 1) * S, :] = v[ROWS : ROWS + S - HALF]
    for j in range(PIECES):
        for o in range(8):
            out[j, o * CROWS : (o + 1) * CROWS, :] = table[o, j * CROWS : (j + 1) * CROWS, :]
        out[j, 8 * CROWS :, :] = mr[j * CROWS : (j + 1) * CROWS, :]
    sent = pltpu.make_async_copy(out, out_hbm, sems.at[9])
    sent.start()
    sent.wait()


def inner_kernel(rate, state, conduct, react, out, coef):
    kap = conduct[0]
    up = (lax.broadcasted_iota(jnp.int32, (S * 8, S), 0) // 8 == lax.broadcasted_iota(jnp.int32, (S * 8, S), 1)).astype(BF16)
    across = (lax.broadcasted_iota(jnp.int32, (S, S * 8), 1) // 8 == lax.broadcasted_iota(jnp.int32, (S, S * 8), 0)).astype(BF16)
    wide = (S * 8, S * 8)
    same = lax.broadcasted_iota(jnp.int32, wide, 0) % 8 == lax.broadcasted_iota(jnp.int32, wide, 1) % 8
    high = react[...].astype(BF16)
    low = (react[...] - high.astype(F32)).astype(BF16)

    def widened(r):
        tall = jnp.dot(up, r, preferred_element_type=F32).astype(BF16)
        return jnp.where(same, jnp.dot(tall, across, preferred_element_type=F32), 0.0).astype(BF16)

    react_hi, react_lo = widened(high), widened(low)
    col = lax.broadcasted_iota(jnp.int32, (B, AREA), 1)
    row = lax.broadcasted_iota(jnp.int32, (B, AREA), 0)
    y, z = col // 32, col % 32
    diag = jnp.zeros((B, AREA), F32)
    for i, (axis, step, at, end) in enumerate(
        ((0, 1, row, 0), (0, B - 1, row, 31), (1, 32, y, 0), (1, AREA - 32, y, 31), (1, 1, z, 0), (1, AREA - 1, z, 31))
    ):
        edge = at == end
        c = 0.5 * (kap + pltpu.roll(kap, step, axis))
        diag = diag + jnp.where(edge, kap, c)
        coef[i] = jnp.where(edge, 0.0, c)
    coef[6] = diag
    for g in range(4):
        x = state[0, :, g * 8 : g * 8 + 8, :].reshape(S * 8, AREA)
        hi = x.astype(BF16)
        lo = (x - hi.astype(F32)).astype(BF16)
        got = jnp.dot(react_hi, hi, preferred_element_type=F32)
        got += jnp.dot(react_hi, lo, preferred_element_type=F32)
        got += jnp.dot(react_lo, hi, preferred_element_type=F32)
        out[0, :, g * 8 : g * 8 + 8, :] = got.reshape(S, 8, AREA)

    def species(s, carry):
        u = state[0, s]
        acc = -coef[6] * u
        for i, (axis, step) in enumerate(((0, 1), (0, B - 1), (1, 32), (1, AREA - 32), (1, 1), (1, AREA - 1))):
            acc = acc + coef[i] * pltpu.roll(u, step, axis)
        out[0, s] = out[0, s] + rate[s] * acc
        return carry

    lax.fori_loop(0, S, species, 0)


def relay_kernel(note, rate, before, own, after, got, out, table):
    j = lax.axis_index("node")
    at = lax.broadcasted_iota(jnp.int32, (CROWS, 128), 0) + CROWS * j
    species = at % S
    first = at // S == (CROWS * j) // S
    rates = jnp.zeros((CROWS, 128), F32)
    for s in range(S):
        rates = jnp.where(species == s, rate[s], rates)
    out[:, FINE + CROWS :, :] = jnp.zeros((PIECES, 8 * CROWS, 128), F32)
    for n in range(PIECES):
        p = note[n, 6]
        c, o = p // 8, (p % 8) * CROWS
        piece = got[c, pl.ds(pl.multiple_of(o, CROWS), CROWS), :]
        out[n, FINE : FINE + CROWS, :] = piece
        kap = jnp.where(first, own[n, 23:24, :], own[n, 35:36, :])
        flux = got[n, 8 * CROWS :, :] - kap * rates * piece
        here = pl.ds(pl.multiple_of(o + FINE + CROWS, 8), CROWS)
        out[c, here, :] = out[c, here, :] + flux
    for g, ref in enumerate((before, own, after)):
        for n in range(PIECES):
            for f in range(6):
                table[g * 96 + n * 6 + f, :ROWS, :] = ref[n, f * ROWS : (f + 1) * ROWS, :]
    for n in range(PIECES):
        for f in range(6):
            q = jnp.maximum(note[n, f], 0)
            out[n, f * ROWS : (f + 1) * ROWS, :] = table[q, :ROWS, :]


def outer_kernel(
    rate, source, got, inner_in, conduct_in, spread_in, place_in, out_hbm, reg_hbm,
    inner, conduct, spread, place, out, reg, crow, cslot, wide, xs, edge, table, sems,
):
    copies = begin(
        sems,
        [(spread_in, spread), (place_in, place), (conduct_in, conduct)]
        + [(inner_in.at[:, lo:hi], inner.at[:, lo:hi]) for lo, hi in CHUNKS],
    )
    for j in range(PIECES):
        crow[j * CROWS : (j + 1) * CROWS, :] = got[j, FINE : FINE + CROWS, :]
        for o in range(8):
            at = FINE + CROWS + o * CROWS
            table[o * 256 + j * CROWS : o * 256 + (j + 1) * CROWS, :] = got[j, at : at + CROWS, :]
    for s in range(S):
        for k2 in range(2):
            for o in range(8):
                reg[0, s, o * 6 : o * 6 + 6, k2 * 128 : k2 * 128 + 128] = table[
                    pl.ds(o * 256 + k2 * S + s, 6, stride=2 * S), :
                ]
    kept = pltpu.make_async_copy(reg, reg_hbm, sems.at[7])
    kept.start()
    copies[0].wait()
    cslot[...] = jnp.zeros_like(cslot)
    for fk in range(12):
        cslot[fk * SLOTS : fk * SLOTS + HALF, :] = crow[fk * S : fk * S + HALF, :]
        cslot[fk * SLOTS + ROWS : fk * SLOTS + ROWS + S - HALF, :] = crow[fk * S + HALF : (fk + 1) * S, :]
    wide[...] = dot(cslot[...], spread[...])
    for k in range(8):
        k2, kk = k // 4, k % 4
        slabs = []
        for f in range(6):
            fine = jnp.concatenate(
                [got[2 * k, f * ROWS : (f + 1) * ROWS, :], got[2 * k + 1, f * ROWS : (f + 1) * ROWS, :]], 0
            )
            at = (f * 2 + k2) * SLOTS
            slabs.append(jnp.where(source[0, f] >= 0, fine, wide[at : at + SLOTS, 128 * kk : 128 * kk + 128]))
        for side in range(2):
            xs[side, :, 128 * k : 128 * k + 128] = slabs[side]
        for q, v in enumerate(swap_blocks(slabs[2:])):
            edge[pl.ds(4 * k + q, SLOTS, stride=32), :] = v
    copies[1].wait()
    copies[2].wait()
    kap = conduct[0]
    row = lax.broadcasted_iota(jnp.int32, (B, AREA), 0)
    done = []
    for i, (lo, hi) in enumerate(CHUNKS):
        ghost = dot(edge[slot(lo) * 32 : (slot(lo) + hi - lo) * 32, :], place[...])
        copies[3 + i].wait()
        for s in range(lo, hi):
            mine = ghost[(s - lo) * 32 : (s - lo + 1) * 32]
            mine = mine + jnp.where(row == 0, xs[0, slot(s) : slot(s) + 1, :], 0.0)
            mine = mine + jnp.where(row == 31, xs[1, slot(s) : slot(s) + 1, :], 0.0)
            out[0, s] = inner[0, s] + rate[s] * (kap * mine)
        c = pltpu.make_async_copy(out.at[:, lo:hi], out_hbm.at[:, lo:hi], sems.at[8 + i])
        c.start()
        done.append(c)
    kept.wait()
    for c in done:
        c.wait()


SPECS = {
    "v": pl.BlockSpec(memory_space=pltpu.VMEM),
    "s": pl.BlockSpec(memory_space=pltpu.SMEM),
    "a": pl.BlockSpec(memory_space=pl.ANY),
}


def call(kernel, ins, outs, spec, scratch, args, limit, copies=0, flops=int(1e9)):
    shapes = [jax.ShapeDtypeStruct(o, F32) for o in outs]
    moved = sum(a.size * a.dtype.itemsize for a in args) + sum(4 * int(np.prod(o)) for o in outs)
    scratch = [x if not isinstance(x, tuple) else pltpu.VMEM(x, F32) for x in scratch]
    return pl.pallas_call(
        kernel,
        out_shape=shapes if len(outs) > 1 else shapes[0],
        in_specs=[SPECS[c] for c in ins],
        out_specs=[SPECS[spec]] * len(outs) if len(outs) > 1 else SPECS[spec],
        scratch_shapes=scratch + ([pltpu.SemaphoreType.DMA((copies,))] if copies else []),
        compiler_params=pltpu.CompilerParams(vmem_limit_bytes=limit << 20),
        cost_estimate=pl.CostEstimate(flops=flops, bytes_accessed=moved, transcendentals=0),
        name=kernel.__name__.removesuffix("_kernel"),
    )(*args)


def shifted(block, distance):
    devices = range(lax.axis_size("sfc"))
    return lax.ppermute(block, "sfc", [(i, i + distance) for i in devices if i + distance in devices])


def exchange(block):
    return lax.all_to_all(block, "node", 0, 0, tiled=True)


def local(fine_state, conduct, spec_rate, reaction, coarse_state, ghost_source, parent_box):
    pick = jnp.asarray(pick_fine(), BF16)
    place = jnp.asarray(pick_fine().T, BF16)
    mean = jnp.asarray(average(), BF16)
    spread = jnp.asarray(4 * average().T, BF16)
    box = (1, S, B, AREA)
    fine, weighted = call(
        pack_fine_kernel,
        "aaaaaa",
        [(PIECES, FINE, 128), (12 * SLOTS, 512)],
        "a",
        [
            pltpu.SMEM((1, 6), jnp.int32), pltpu.SMEM((1,), jnp.int32), box, (1, B, AREA),
            pltpu.VMEM((AREA, 128), BF16), pltpu.VMEM((512, 128), BF16), (PIECES, FINE, 128), (12 * SLOTS, 512),
            (SLOTS * 32, 128), (2, SLOTS, AREA), (16, 512),
        ],
        (ghost_source, parent_box, fine_state, conduct, pick, mean),
        58,
        11,
    )
    own = exchange(fine)
    coarse = call(
        pack_coarse_kernel,
        "aaaaaaa",
        [(PIECES, 9 * CROWS, 128)],
        "a",
        [
            pltpu.SMEM((S,), F32), pltpu.SMEM((1, 6), jnp.int32), box, (12 * SLOTS, 512),
            pltpu.VMEM((AREA, 256), BF16), pltpu.VMEM((256, 256), BF16), pltpu.VMEM((512, 128), BF16),
            (PIECES, 9 * CROWS, 128), (2, S * 32, 128), (4 * SLOTS, AREA), (8, 256, 128), (256, 128),
        ],
        (spec_rate, ghost_source, coarse_state, weighted, jnp.asarray(pick_coarse(), BF16), jnp.asarray(split_octants(), BF16), mean),
        58,
        10,
    )
    grouped = exchange(coarse)
    before, after = shifted(own, 1), shifted(own, -1)
    inner = call(inner_kernel, "svvv", [box], "v", [(7, B, AREA)], (spec_rate, fine_state, conduct, reaction), 24)
    note = own[:, 11, :8].astype(jnp.int32)
    before, inner = lax.optimization_barrier((before, inner))
    chosen = call(
        relay_kernel,
        "ssvvvv",
        [(PIECES, FINE + 9 * CROWS, 128)],
        "v",
        [(3 * 96, ROWS, 128)],
        (note, spec_rate, before, own, after, grouped),
        24,
    )
    mine = exchange(chosen)
    tendency, register = call(
        outer_kernel,
        "ssvaaaa",
        [box, (1, S, 48, 256)],
        "a",
        [
            box, (1, B, AREA), pltpu.VMEM((128, 512), BF16), pltpu.VMEM((128, AREA), BF16), box, (1, S, 48, 256),
            (256, 128), (12 * SLOTS, 128), (12 * SLOTS, 512), (2, SLOTS, AREA), (SLOTS * 32, 128), (8 * 256, 128),
        ],
        (spec_rate, ghost_source, mine, inner, conduct, spread, place),
        32,
        12,
    )
    return tendency, register.transpose(0, 2, 1, 3)


def solution(mesh):
    box = P(("sfc", "node"))
    return jax.shard_map(
        local,
        mesh=mesh,
        in_specs=(box, box, P(), P(), box, box, box),
        out_specs=(box, box),
        check_vma=False,
    )
```

time: 95.4 us -> 87.7 us (0.919)
  blocking collectives: 15.8 us -> 30.1 us
  local copies, waits for them, and re-layouts: 14.8 us -> 3.69 us
  waiting for transfers between devices: 22.5 us -> 11.6 us
  Pallas kernels: 18 us -> 24.2 us
  starting transfers between devices: 19.9 us -> 15.2 us
  other arithmetic: 2.26 us -> 0.01 us
    all_to_all x1, blocking collectives: 15.8 us -> 30.1 us  [exchange(): return lax.all_to_all(block, 'node', 0, 0, tiled=True)]
    all_to_all x3 -> x2, waiting for transfers between devices: 22.5 us -> 11.6 us  [exchange(): return lax.all_to_all(block, 'node', 0, 0, tiled=True)]
    unnamed x37 -> x18, local copies, waits for them, and re-layouts: 11.8 us -> 3.69 us
    pallas_call x7 -> x5, Pallas kernels: 18 us -> 24.2 us  [call(): pl.pallas_call(kernel, out_shape=shapes if len(outs) > 1 else shapes[0],...]
    all_to_all x3 -> x2, starting transfers between devices: 15.5 us -> 12.5 us  [exchange(): return lax.all_to_all(block, 'node', 0, 0, tiled=True)]
    mul x1 -> x0, local copies, waits for them, and re-layouts: 2.18 us -> none  [local(): react = jnp.kron(reaction, jnp.eye(8, dtype=F32))]
    ppermute x2, starting transfers between devices: 4.36 us -> 2.62 us  [shifted(): lax.ppermute(block, 'sfc', [(i, i + distance) for i in devices if i + dis...]
    mul x1 -> x0, other arithmetic: 1.51 us -> none  [local(): react = jnp.kron(reaction, jnp.eye(8, dtype=F32))]
  transfers between devices with their start and end apart: 5 -> 4, of which waited for: 3 -> 2; matrix products, arithmetic and copies ran while one was open for 4% -> 0% of each run, Pallas kernels for 16% -> 15%
where the time goes in v1:
time: 87.7 us; the launch traced here: 86.2 us
  blocking collectives  30.1 us (34%)
  Pallas kernels  24.2 us (28%)
  starting transfers between devices  15.2 us (17%)
  waiting for transfers between devices  11.6 us (13%)
  local copies, waits for them, and re-layouts  3.69 us (4%)
  between operations  1.45 us (2%)
    all_to_all x1, blocking collectives, exchange(): return lax.all_to_all(block, 'node', 0, 0, tiled=True)  30.1 us
    pallas_call x5, Pallas kernels, call(): pl.pallas_call(kernel, out_shape=shapes if len(outs) > 1 else shapes[0],...  24.2 us
    all_to_all x2, starting transfers between devices, exchange(): return lax.all_to_all(block, 'node', 0, 0, tiled=True)  12.5 us
    all_to_all x2, waiting for transfers between devices, exchange(): return lax.all_to_all(block, 'node', 0, 0, tiled=True)  11.6 us
    unnamed x18, local copies, waits for them, and re-layouts  3.69 us
    ppermute x2, starting transfers between devices, shifted(): lax.ppermute(block, 'sfc', [(i, i + distance) for i in devices if i + dis...  2.62 us
  transfers between devices with their start and end apart: 4, of which 2 were waited for; matrix products, arithmetic and copies ran while one was open for 0% of the time, Pallas kernels for 15%

profile of v1, /device:TPU:0, one launch (start us, length us, event | category | flops | bytes accessed | tf_op | source)
XLA Modules:
  0.0 86.2 jit_solution(16499065883652796052)
XLA Ops:
  1.3 4.0 %pack_fine.1 = (f32[16,72,128]{2,1,0:T(8,128)}, f32[288,512]{1,0:T(8,128)}) custom-call(s32[1,6]{1,0:T(1,128)} %source.1, s32[1]{0:T(128)S(6)} %copy.20.parent_in, f32[1,21,32,1024]{3,2,1,0:T(8,128)} %state.1, f32[1,32,1024]{2,1,0:T(8,128)} %conduct_in.3, bf16[1024,128]{1,0:T(8,128)(2,1)} %constant.12.clone.pick_in, bf16[512,128]{1,0:T(8,128)(2,1)} %constant.14.clone.mean_in), custom_call_target="tpu_custom_call" | custom-call | flops 1000000000 | bytes 4456476 | tf_op jit(solution)/shard_map/pack_fine/pallas_call | solution.py:381
  5.2 8.1 %all-to-all-start = ((f32[16,72,128]{2,1,0:T(8,128)}), f32[16,72,128]{2,1,0:T(8,128)S(1)}, u32[]{:S(2)}, u32[]{:S(2)}) async-start(f32[16,72,128]{2,1,0:T(8,128)} %get-tuple-element.8), calls=%async_computation | async-start | bytes 1179648 | tf_op jit(solution)/shard_map/all_to_all | solution.py:399
  13.4 0.0 copy-start.3
  13.4 0.0 copy-start.6
  13.4 0.0 copy-start.7
  13.4 6.4 %pack_coarse.1 = f32[16,144,128]{2,1,0:T(8,128)} custom-call(f32[21]{0:T(128)} %rate.5, s32[1,6]{1,0:T(1,128)} %source.1, f32[1,21,32,1024]{3,2,1,0:T(8,128)} %coarse_in.1, f32[288,512]{1,0:T(8,128)} %get-tuple-element.10.weighted_in, bf16[1024,256]{1,0:T(8,128)(2,1)} %constant.16.clone.pick_in, bf16[256,256]{1,0:T(8,128)(2,1)} %constant.17.clone.octs_in, ...), custom_call_target="tpu_custom_call" | custom-call | flops 1000000000 | bytes 5308524 | tf_op jit(solution)/shard_map/pack_coarse/pallas_call | solution.py:381
  19.8 5.8 %all-to-all-done.own = f32[16,72,128]{2,1,0:T(8,128)S(1)} async-done(((f32[16,72,128]{2,1,0:T(8,128)}), f32[16,72,128]{2,1,0:T(8,128)S(1)}, u32[]{:S(2)}, u32[]{:S(2)}) %all-to-all-start) | async-done | bytes 589856 | tf_op jit(solution)/shard_map/all_to_all | solution.py:399
  25.6 4.4 %all-to-all-start.1 = ((f32[16,144,128]{2,1,0:T(8,128)}), f32[16,144,128]{2,1,0:T(8,128)}, u32[]{:S(2)}, u32[]{:S(2)}) async-start(f32[16,144,128]{2,1,0:T(8,128)} %pack_coarse.1), calls=%async_computation.1 | async-start | bytes 2359296 | tf_op jit(solution)/shard_map/all_to_all | solution.py:399
  30.0 1.3 %collective-permute-start = (f32[16,72,128]{2,1,0:T(8,128)S(1)}, f32[16,72,128]{2,1,0:T(8,128)S(1)}, u32[]{:S(2)}, u32[]{:S(2)}) collective-permute-start(f32[16,72,128]{2,1,0:T(8,128)S(1)} %all-to-all-done.own), channel_id=1, source_target_pairs={{0,16},{16,32},{32,48},{48,64},{64,80},{80,96},{96,112},{1,17},{17... | collective-permute-start | bytes 1769480 | tf_op jit(solution)/shard_map/ppermute | solution.py:395
  31.4 1.3 %collective-permute-start.1 = (f32[16,72,128]{2,1,0:T(8,128)S(1)}, f32[16,72,128]{2,1,0:T(8,128)}, u32[]{:S(2)}, u32[]{:S(2)}) collective-permute-start(f32[16,72,128]{2,1,0:T(8,128)S(1)} %all-to-all-done.own), channel_id=1, source_target_pairs={{16,0},{32,16},{48,32},{64,48},{80,64},{96,80},{112,96},{17,1},{33... | collective-permute-start | bytes 1769480 | tf_op jit(solution)/shard_map/ppermute | solution.py:395
  32.7 0.0 copy-done.3
  32.7 0.0 copy-done.6
  32.7 0.0 copy-done.7
  32.7 0.0 copy-start
  32.7 1.8 %copy-done = f32[1,21,32,1024]{3,2,1,0:T(8,128)S(1)} copy-done((f32[1,21,32,1024]{3,2,1,0:T(8,128)S(1)}, f32[1,21,32,1024]{3,2,1,0:T(8,128)}, u32[]{:S(2)}) %copy-start) | copy-done | bytes 2752536
  34.5 6.7 %inner.1.inner_in = f32[1,21,32,1024]{3,2,1,0:T(8,128)S(1)} custom-call(f32[21]{0:T(128)S(1)} %copy-done.7, f32[1,21,32,1024]{3,2,1,0:T(8,128)S(1)} %copy-done, f32[1,32,1024]{2,1,0:T(8,128)S(1)} %copy-done.3, f32[21,21]{1,0:T(8,128)S(1)} %copy-done.6), custom_call_target="tpu_custom_call" | custom-call | flops 1000000000 | bytes 5637944 | tf_op jit(solution)/shard_map/inner/pallas_call | solution.py:381
  41.2 0.0 collective-permute-done.before
  41.2 0.0 copy-start.1
  41.2 0.8 copy-done.1
  42.0 5.8 %all-to-all-done.1.got = f32[16,144,128]{2,1,0:T(8,128)} async-done(((f32[16,144,128]{2,1,0:T(8,128)}), f32[16,144,128]{2,1,0:T(8,128)}, u32[]{:S(2)}, u32[]{:S(2)}) %all-to-all-start.1) | async-done | bytes 1179680 | tf_op jit(solution)/shard_map/all_to_all | solution.py:399
  47.8 0.0 collective-permute-done.1.after
  47.8 0.0 copy-start.2
  47.8 1.1 %copy-done.2 = f32[16,72,128]{2,1,0:T(8,128)S(1)} copy-done((f32[16,72,128]{2,1,0:T(8,128)S(1)}, f32[16,72,128]{2,1,0:T(8,128)}, u32[]{:S(2)}) %copy-start.2) | copy-done | bytes 589848
  48.9 1.9 %relay.1 = f32[16,216,128]{2,1,0:T(8,128)S(1)} custom-call(s32[16,8]{1,0:T(8,128)S(1)} %bitcast.2, f32[21]{0:T(128)S(1)} %copy-done.7, f32[16,72,128]{2,1,0:T(8,128)S(1)} %copy-done.2, f32[16,72,128]{2,1,0:T(8,128)S(1)} %all-to-all-done.own, f32[16,72,128]{2,1,0:T(8,128)} %collective-permute-done.1.after, f32[16,144,128]{2,1,0:T(8,128)} %all-to-all-done.1.got), custom_call_target="tpu_custom_call" | custom-call | flops 1000000000 | bytes 4719188 | tf_op jit(solution)/shard_map/relay/pallas_call | solution.py:381
  50.8 0.0 copy-start.4
  50.8 0.0 copy-start.5
  50.8 0.0 copy-start.8
  50.8 30.1 %all_to_all.15.got = f32[16,216,128]{2,1,0:T(8,128)S(1)} all-to-all(f32[16,216,128]{2,1,0:T(8,128)S(1)} %relay.1), channel_id=1, replica_groups=mesh['sfc'=8,'node'=16] {'node'}, dimensions={0} | all-to-all | bytes 3538944 | tf_op jit(solution)/shard_map/all_to_all | solution.py:399
  80.9 0.0 copy-done.4
  80.9 0.0 copy-done.5
  80.9 0.0 copy-done.8
  81.0 5.3 %outer.1 = (f32[1,21,32,1024]{3,2,1,0:T(8,128)}, f32[1,21,48,256]{3,2,1,0:T(8,128)}) custom-call(f32[21]{0:T(128)S(1)} %copy-done.7, s32[1,6]{1,0:T(1,128)S(1)} %copy-done.8, f32[16,216,128]{2,1,0:T(8,128)S(1)} %all_to_all.15.got, f32[1,21,32,1024]{3,2,1,0:T(8,128)S(1)} %inner.1.inner_in, f32[1,32,1024]{2,1,0:T(8,128)S(1)} %copy-done.3, ...), custom_call_target="tpu_custom_call" | custom-call | flops 1000000000 | bytes 8831084 | tf_op jit(solution)/shard_map/outer/pallas_call | solution.py:381
  (1 shorter events, 0.0 us)
Async XLA Ops:
  5.2 20.4 %all-to-all-start = ((f32[16,72,128]{2,1,0:T(8,128)}), f32[16,72,128]{2,1,0:T(8,128)S(1)}, u32[]{:S(2)}, u32[]{:S(2)}) async-start(f32[16,72,128]{2,1,0:T(8,128)} %get-tuple-element.8), calls=%async_computation | async-start | bytes 1179648 | tf_op jit(solution)/shard_map/all_to_all | solution.py:399
  13.4 19.3 %copy-start.3 = (f32[1,32,1024]{2,1,0:T(8,128)S(1)}, f32[1,32,1024]{2,1,0:T(8,128)}, u32[]{:S(2)}) copy-start(f32[1,32,1024]{2,1,0:T(8,128)} %conduct_in.3) | copy-start | bytes 393220
  13.4 19.3 %copy-start.6 = (f32[21,21]{1,0:T(8,128)S(1)}, f32[21,21]{1,0:T(8,128)}, u32[]{:S(2)}) copy-start(f32[21,21]{1,0:T(8,128)} %react.1) | copy-start | bytes 5296
  13.4 19.3 %copy-start.7 = (f32[21]{0:T(128)S(1)}, f32[21]{0:T(128)}, u32[]{:S(2)}) copy-start(f32[21]{0:T(128)} %rate.5) | copy-start | bytes 256
  25.6 22.2 %all-to-all-start.1 = ((f32[16,144,128]{2,1,0:T(8,128)}), f32[16,144,128]{2,1,0:T(8,128)}, u32[]{:S(2)}, u32[]{:S(2)}) async-start(f32[16,144,128]{2,1,0:T(8,128)} %pack_coarse.1), calls=%async_computation.1 | async-start | bytes 2359296 | tf_op jit(solution)/shard_map/all_to_all | solution.py:399
  30.0 11.1 %collective-permute-start = (f32[16,72,128]{2,1,0:T(8,128)S(1)}, f32[16,72,128]{2,1,0:T(8,128)S(1)}, u32[]{:S(2)}, u32[]{:S(2)}) collective-permute-start(f32[16,72,128]{2,1,0:T(8,128)S(1)} %all-to-all-done.own), channel_id=1, source_target_pairs={{0,16},{16,32},{32,48},{48,64},{64,80},{80,96},{96,112},{1,17},{17... | collective-permute-start | bytes 1769480 | tf_op jit(solution)/shard_map/ppermute | solution.py:395
  31.4 16.5 %collective-permute-start.1 = (f32[16,72,128]{2,1,0:T(8,128)S(1)}, f32[16,72,128]{2,1,0:T(8,128)}, u32[]{:S(2)}, u32[]{:S(2)}) collective-permute-start(f32[16,72,128]{2,1,0:T(8,128)S(1)} %all-to-all-done.own), channel_id=1, source_target_pairs={{16,0},{32,16},{48,32},{64,48},{80,64},{96,80},{112,96},{17,1},{33... | collective-permute-start | bytes 1769480 | tf_op jit(solution)/shard_map/ppermute | solution.py:395
  32.7 1.8 %copy-start = (f32[1,21,32,1024]{3,2,1,0:T(8,128)S(1)}, f32[1,21,32,1024]{3,2,1,0:T(8,128)}, u32[]{:S(2)}) copy-start(f32[1,21,32,1024]{3,2,1,0:T(8,128)} %state.1) | copy-start | bytes 8257540
  41.2 0.8 copy-start.1
  47.8 1.1 %copy-start.2 = (f32[16,72,128]{2,1,0:T(8,128)S(1)}, f32[16,72,128]{2,1,0:T(8,128)}, u32[]{:S(2)}) copy-start(f32[16,72,128]{2,1,0:T(8,128)} %copy-done.1) | copy-start | bytes 1769476
  50.8 30.1 %copy-start.4 = (bf16[128,1024]{1,0:T(8,128)(2,1)S(1)}, bf16[128,1024]{1,0:T(8,128)(2,1)}, u32[]{:S(2)}) copy-start(bf16[128,1024]{1,0:T(8,128)(2,1)} %constant.13.clone.place_in) | copy-start | bytes 786436
  50.8 30.1 %copy-start.5 = (bf16[128,512]{1,0:T(8,128)(2,1)S(1)}, bf16[128,512]{1,0:T(8,128)(2,1)}, u32[]{:S(2)}) copy-start(bf16[128,512]{1,0:T(8,128)(2,1)} %constant.15.clone.spread_in) | copy-start | bytes 393220
  50.8 30.1 %copy-start.8 = (s32[1,6]{1,0:T(1,128)S(1)}, s32[1,6]{1,0:T(1,128)}, u32[]{:S(2)}) copy-start(s32[1,6]{1,0:T(1,128)} %source.1) | copy-start | bytes 76

commit v2 on v1

v2 whole, which is shorter than its diff:
```python
import functools

import jax
import jax.numpy as jnp
import numpy as np
from jax import lax
from jax.experimental import pallas as pl
from jax.experimental.pallas import tpu as pltpu
from jax.sharding import PartitionSpec as P

S, B, AREA = 21, 32, 1024
PIECES = 16
HALF = 11
SLOTS = 24
ROWS = 12
FINE = 6 * ROWS
PART = 3
FACE = 48
CAP = 16
LIST = CAP * PART
MEANS = 24
F32, BF16 = jnp.float32, jnp.bfloat16


def slot(s):
    return s if s < HALF else s + 1


def pick_fine():
    m = np.zeros((AREA, 128), np.float32)
    for b in range(32):
        m[b, b] = 1
        m[31 * 32 + b, 32 + b] = 1
        m[b * 32, 64 + b] = 1
        m[b * 32 + 31, 96 + b] = 1
    return m


def pick_coarse():
    m = np.zeros((AREA, 256), np.float32)
    for w, p in enumerate((0, 15, 16, 31)):
        for b in range(32):
            m[p * 32 + b, w * 32 + b] = 1
            m[b * 32 + p, 128 + w * 32 + b] = 1
    return m


def split_octants():
    m = np.zeros((256, 256), np.float32)
    for a in range(8):
        for o in range(2):
            for b in range(16):
                m[a * 32 + o * 16 + b, o * 128 + a * 16 + b] = 1
    return m


def average():
    m = np.zeros((512, 128), np.float32)
    for a in range(16):
        for b in range(32):
            m[a * 32 + b, (a // 2) * 16 + b // 2] = 0.25
    return m


def dot(x, m):
    hi = x.astype(BF16)
    lo = (x - hi.astype(F32)).astype(BF16)
    return jnp.dot(hi, m, preferred_element_type=F32) + jnp.dot(lo, m, preferred_element_type=F32)


def dot_twice(x, m):
    hi = x.astype(BF16)
    lo = (x - hi.astype(F32)).astype(BF16)
    return jnp.dot(jnp.concatenate([hi, lo], 1), m, preferred_element_type=F32)


def lanes(rows):
    return lax.broadcasted_iota(jnp.int32, (rows, 128), 1)


def swap_blocks(parts):
    block = lanes(parts[0].shape[0]) // 32
    out = []
    for f in range(4):
        acc = None
        for q in range(4):
            moved = parts[q] if q == f else pltpu.roll(parts[q], (32 * (q - f)) % 128, 1)
            acc = moved if acc is None else jnp.where(block == q, moved, acc)
        out.append(acc)
    return out


CHUNKS = ((0, 6), (6, 11), (11, 16), (16, 21))


def begin(sems, pairs):
    copies = [pltpu.make_async_copy(src, dst, sems.at[i]) for i, (src, dst) in enumerate(pairs)]
    for c in copies:
        c.start()
    return copies


def pack_fine_kernel(
    source_in, parent_in, state_in, conduct_in, pick_in, fine_out, weighted_out,
    source, parent, state, conduct, pick, fine, weighted, edge, xs, sems,
):
    copies = begin(
        sems,
        [(pick_in, pick), (conduct_in, conduct)]
        + [(state_in.at[:, lo:hi], state.at[:, lo:hi]) for lo, hi in CHUNKS]
        + [(source_in, source), (parent_in, parent)],
    )
    edge[HALF * 32 : HALF * 32 + 32, :] = jnp.zeros((32, 128), F32)
    edge[22 * 32 : 23 * 32, :] = jnp.zeros((32, 128), F32)
    for side in range(2):
        for r in (11, 22):
            xs[side, r : r + 1, :] = jnp.zeros((1, AREA), F32)
    copies[0].wait()
    copies[1].wait()
    sel = pick[...]
    edge[23 * 32 : 24 * 32, :] = dot(conduct[0], sel)
    xs[0, 23:24, :] = conduct[0, 0:1, :]
    xs[1, 23:24, :] = conduct[0, 31:32, :]
    for i, (lo, hi) in enumerate(CHUNKS):
        copies[2 + i].wait()
        got = dot(state[0, lo:hi].reshape((hi - lo) * 32, AREA), sel)
        edge[slot(lo) * 32 : (slot(lo) + hi - lo) * 32, :] = got
        for s in range(lo, hi):
            xs[0, slot(s) : slot(s) + 1, :] = state[0, s, 0:1, :]
            xs[1, slot(s) : slot(s) + 1, :] = state[0, s, 31:32, :]
    row = lax.broadcasted_iota(jnp.int32, (SLOTS, 128), 0)
    for c in copies[6:]:
        c.wait()
    lane = lanes(1)
    note = jnp.where(lane == 6, parent[0], 0)
    for f in range(6):
        note = jnp.where(lane == f, source[0, f], note)
    note = note.astype(F32)
    sent = []
    for k in range(8):
        across = [xs[side, :, 128 * k : 128 * k + 128] for side in range(2)]
        across += swap_blocks([edge[pl.ds(4 * k + q, SLOTS, stride=32), :] for q in range(4)])
        k2, kk = k // 4, k % 4
        for f in range(6):
            t = across[f]
            fine[2 * k, f * ROWS : (f + 1) * ROWS, :] = t[:ROWS]
            fine[2 * k + 1, f * ROWS : (f + 1) * ROWS, :] = t[ROWS:]
            at = f * 2 + k2
            kap = jnp.broadcast_to(t[23:24], (SLOTS, 128))
            weighted[at * SLOTS : (at + 1) * SLOTS, 128 * kk : 128 * kk + 128] = jnp.where(row == 23, t, t * kap)
        for j in (2 * k, 2 * k + 1):
            fine[j, 11:12, :] = note
        c = pltpu.make_async_copy(fine.at[2 * k : 2 * k + 2], fine_out.at[2 * k : 2 * k + 2], sems.at[8 + k])
        c.start()
        sent.append(c)
    c = pltpu.make_async_copy(weighted, weighted_out, sems.at[16])
    c.start()
    for c in sent + [c]:
        c.wait()


def turn(x):
    n = x.shape[0] // 8
    x = x.reshape(n, 8, 128)
    row = lax.broadcasted_iota(jnp.int32, (n, 8, 128), 1)
    group = lax.broadcasted_iota(jnp.int32, (n, 8, 128), 2) // 16
    for d in (1, 2, 4):
        up = pltpu.roll(pltpu.roll(x, 8 - d, 1), 16 * d, 2)
        down = pltpu.roll(pltpu.roll(x, d, 1), 128 - 16 * d, 2)
        rb, gb = row & d, group & d
        x = jnp.where(rb == gb, x, jnp.where(rb == 0, up, down))
    return x.reshape(n * 8, 128)


def pack_coarse_kernel(
    rate_in, source_in, coarse_in, weighted_in, pick_in, octs_in, mean_in, packed_out, first_out, second_out,
    rate, source, coarse, weighted, pick, octs, mean, turned, planes, packed, first, second, sems,
):
    copies = begin(
        sems,
        [(pick_in, pick)]
        + [(coarse_in.at[:, lo : lo + 7], coarse.at[:, lo : lo + 7]) for lo in range(0, S, 7)]
        + [(octs_in, octs), (mean_in, mean), (weighted_in, weighted), (rate_in, rate), (source_in, source)],
    )
    copies[0].wait()
    sel = pick[...]
    for i, lo in enumerate(range(0, S, 7)):
        copies[1 + i].wait()
        got = dot(coarse[0, lo : lo + 7].reshape(224, AREA), sel)
        for t in range(2):
            for s in range(7):
                turned[t, (lo + s) * 32 : (lo + s + 1) * 32, :] = turn(got[s * 32 : s * 32 + 32, 128 * t : 128 * t + 128])
    for c in copies[4:]:
        c.wait()
    planes[...] = jnp.zeros_like(planes)
    for w, p in enumerate((0, 15, 16, 31)):
        for s in range(S):
            planes[w * SLOTS + s : w * SLOTS + s + 1, :] = coarse[0, s, p : p + 1, :]
    for at in range(48):
        packed[at * FACE + 2 * S : (at + 1) * FACE, :] = jnp.zeros((FACE - 2 * S, 128), F32)
    for oy in range(2):
        for k2 in range(2):
            c = oy * 2 + k2
            got = dot(planes[:, 256 * c : 256 * c + 256], octs[...])
            for w in range(4):
                for oz in range(2):
                    at = (4 * (w // 2) + 2 * oy + oz) * 6 + w % 2
                    at = at * FACE + k2 * S
                    packed[at : at + S, :] = got[w * SLOTS : w * SLOTS + S, oz * 128 : oz * 128 + 128]
    for t in range(2):
        for g in range(4):
            ox, k2 = g // 2, g % 2
            for w in range(4):
                for i in range(2):
                    oy, oz = (w // 2, i) if t == 0 else (i, w // 2)
                    f = 2 + 2 * t + w % 2
                    at = ((4 * ox + 2 * oy + oz) * 6 + f) * FACE + k2 * S
                    packed[at : at + S, :] = turned[
                        t, pl.ds(g * 8 + w * 2 + i, S, stride=32), :
                    ]
    saved = []
    row = lax.broadcasted_iota(jnp.int32, (SLOTS, 128), 0)
    rates = jnp.zeros((SLOTS, 128), F32)
    for s in range(S):
        rates = jnp.where(row == slot(s), rate[s], rates)
    averaged = dot(weighted[...], mean[...])
    for f in range(6):
        keep = jnp.where(source[0, f] < 0, 1.0, 0.0)
        for ref in (first, second):
            ref[f, 2 * S :, :] = jnp.zeros((FACE - 2 * S, 128), F32)
        for k2 in range(2):
            v = averaged[(f * 2 + k2) * SLOTS : (f * 2 + k2 + 1) * SLOTS] * keep
            kap = v[23:24]
            for ref, w in ((first, v * rates), (second, jnp.broadcast_to(kap, (SLOTS, 128)) * rates)):
                ref[f, k2 * S : k2 * S + HALF, :] = w[:HALF]
                ref[f, k2 * S + HALF : (k2 + 1) * S, :] = w[ROWS : ROWS + S - HALF]
            for j in range(7 * k2, 7 * k2 + (7 if k2 == 0 else 9)):
                at = 48 * FACE + j * MEANS + 18 + f
                packed[at : at + 1, :] = kap
        for j in range(PIECES):
            at = 48 * FACE + j * MEANS + PART * f
            packed[at : at + PART, :] = first[f, PART * j : PART * j + PART, :]
    for i, (src, dst) in enumerate(((packed, packed_out), (first, first_out), (second, second_out))):
        c = pltpu.make_async_copy(src, dst, sems.at[9 + i])
        c.start()
        saved.append(c)
    for c in saved:
        c.wait()


def choose_kernel(note, packed, out_hbm, mine, out, count, sems):
    me = lax.axis_index("node")
    count[0] = 0
    for n in range(PIECES):
        p = note[n, 6]

        @pl.when(p // 8 == me)
        def _(n=n, p=p):
            at = count[0]
            for f in range(6):
                hit = note[n, f] < 0
                mine[jnp.where(hit, jnp.minimum(at, CAP), CAP)] = (p % 8) * 6 + f
                at = at + hit.astype(jnp.int32)
            count[0] = at

    for i in range(CAP):
        mine[i] = jnp.where(i < count[0], mine[i], 48)
        face = packed[pl.ds(pl.multiple_of(jnp.minimum(mine[i], 47) * FACE, 8), FACE), :]
        for j in range(PIECES):
            out[j, PART * i : PART * i + PART, :] = face[PART * j : PART * j + PART]
    for j in range(PIECES):
        out[j, LIST:, :] = packed[48 * FACE + j * MEANS : 48 * FACE + (j + 1) * MEANS, :]
    sent = pltpu.make_async_copy(out, out_hbm, sems.at[0])
    sent.start()
    sent.wait()


def inner_kernel(rate, state, conduct, react, later, out, coef):
    del later
    kap = conduct[0]
    up = (lax.broadcasted_iota(jnp.int32, (S * 8, S), 0) // 8 == lax.broadcasted_iota(jnp.int32, (S * 8, S), 1)).astype(BF16)
    across = (lax.broadcasted_iota(jnp.int32, (S, S * 8), 1) // 8 == lax.broadcasted_iota(jnp.int32, (S, S * 8), 0)).astype(BF16)
    wide = (S * 8, S * 8)
    same = lax.broadcasted_iota(jnp.int32, wide, 0) % 8 == lax.broadcasted_iota(jnp.int32, wide, 1) % 8
    high = react[...].astype(BF16)
    low = (react[...] - high.astype(F32)).astype(BF16)

    def widened(r):
        tall = jnp.dot(up, r, preferred_element_type=F32).astype(BF16)
        return jnp.where(same, jnp.dot(tall, across, preferred_element_type=F32), 0.0).astype(BF16)

    react_hi, react_lo = widened(high), widened(low)
    col = lax.broadcasted_iota(jnp.int32, (B, AREA), 1)
    row = lax.broadcasted_iota(jnp.int32, (B, AREA), 0)
    y, z = col // 32, col % 32
    diag = jnp.zeros((B, AREA), F32)
    for i, (axis, step, at, end) in enumerate(
        ((0, 1, row, 0), (0, B - 1, row, 31), (1, 32, y, 0), (1, AREA - 32, y, 31), (1, 1, z, 0), (1, AREA - 1, z, 31))
    ):
        edge = at == end
        c = 0.5 * (kap + pltpu.roll(kap, step, axis))
        diag = diag + jnp.where(edge, kap, c)
        coef[i] = jnp.where(edge, 0.0, c)
    coef[6] = diag
    for g in range(4):
        x = state[0, :, g * 8 : g * 8 + 8, :].reshape(S * 8, AREA)
        hi = x.astype(BF16)
        lo = (x - hi.astype(F32)).astype(BF16)
        got = jnp.dot(react_hi, hi, preferred_element_type=F32)
        got += jnp.dot(react_hi, lo, preferred_element_type=F32)
        got += jnp.dot(react_lo, hi, preferred_element_type=F32)
        out[0, :, g * 8 : g * 8 + 8, :] = got.reshape(S, 8, AREA)

    def species(s, carry):
        u = state[0, s]
        acc = -coef[6] * u
        for i, (axis, step) in enumerate(((0, 1), (0, B - 1), (1, 32), (1, AREA - 32), (1, 1), (1, AREA - 1))):
            acc = acc + coef[i] * pltpu.roll(u, step, axis)
        out[0, s] = out[0, s] + rate[s] * acc
        return carry

    lax.fori_loop(0, S, species, 0)


def relay_kernel(note, rate, before, own, after, got, out_hbm, over, out, table, listed, fluxes, seen, sems):
    for c in range(PIECES):
        seen[c] = 0
    j = lax.axis_index("node")
    species = (lax.broadcasted_iota(jnp.int32, (PART, 128), 0) + PART * j) % S
    rates = jnp.zeros((PART, 128), F32)
    for s in range(S):
        rates = jnp.where(species == s, rate[s], rates)
    for c in range(PIECES):
        for i in range(CAP):
            listed[c * CAP + i, :PART, :] = got[c, PART * i : PART * i + PART, :]
    for g, ref in enumerate((before, own, after)):
        for n in range(PIECES):
            for f in range(6):
                table[g * 96 + n * 6 + f, :ROWS, :] = ref[n, f * ROWS : (f + 1) * ROWS, :]
    for n in range(PIECES):
        c = note[n, 6] // 8
        place = seen[c]
        for f in range(6):
            q = note[n, f]
            rank = jnp.where(q < 0, jnp.minimum(place, CAP), CAP)
            place = jnp.where(q < 0, place + 1, place)
            fine = table[jnp.maximum(q, 0), :ROWS, :]
            e = c * CAP + jnp.minimum(rank, CAP - 1)
            piece = listed[e, :PART, :]
            out[n, f * ROWS + PART : (f + 1) * ROWS, :] = fine[PART:]
            out[n, f * ROWS : f * ROWS + PART, :] = jnp.where(q >= 0, fine[:PART], piece)
            kap = got[n, LIST + 18 + f : LIST + 19 + f, :]
            flux = got[n, LIST + PART * f : LIST + PART * f + PART, :] - kap * rates * piece
            fluxes[jnp.where(rank < CAP, e, PIECES * CAP), :PART, :] = flux
        seen[c] = place
    most = seen[0]
    for c in range(1, PIECES):
        most = jnp.maximum(most, seen[c])
    over[0] = (most > CAP).astype(jnp.int32)
    for c in range(PIECES):
        for i in range(CAP):
            out[c, FINE + PART * i : FINE + PART * i + PART, :] = fluxes[c * CAP + i, :PART, :]
    sent = pltpu.make_async_copy(out, out_hbm, sems.at[0])
    sent.start()
    sent.wait()


def outer_kernel(
    rate, source, listed, over, got, inner_in, conduct_in, spread_in, place_in, ghost_in, rows_in, out_hbm, reg_hbm,
    inner, conduct, spread, place, out, reg, crow, cslot, wide, xs, edge, table, held, sems,
):
    copies = begin(
        sems,
        [(spread_in, spread), (place_in, place), (conduct_in, conduct)]
        + [(inner_in.at[:, lo:hi], inner.at[:, lo:hi]) for lo, hi in CHUNKS],
    )
    table[...] = jnp.zeros_like(table)
    for i in range(CAP):
        held[i, 2 * S :, :] = jnp.zeros((FACE - 2 * S, 128), F32)
    for j in range(14):
        at = slice(PART * j, PART * j + PART)
        for f in range(6):
            crow[f, at, :] = got[j, f * ROWS : f * ROWS + PART, :]
        for i in range(CAP):
            held[i, at, :] = got[j, FINE + PART * i : FINE + PART * i + PART, :]
    for i in range(CAP):
        face = pl.ds(pl.multiple_of(listed[i] * FACE, 8), FACE)
        table[face, :] = table[face, :] + held[i]

    @pl.when(over[0] > 0)
    def _():
        for src, dst, sem in ((ghost_in, crow, sems.at[12]), (rows_in, table.at[: 48 * FACE], sems.at[13])):
            c = pltpu.make_async_copy(src, dst, sem)
            c.start()
            c.wait()

    for s in range(S):
        for k2 in range(2):
            reg[0, s, :, k2 * 128 : k2 * 128 + 128] = table[pl.ds(k2 * S + s, 48, stride=FACE), :]
    kept = pltpu.make_async_copy(reg, reg_hbm, sems.at[7])
    kept.start()
    copies[0].wait()
    cslot[...] = jnp.zeros_like(cslot)
    for fk in range(12):
        at = fk % 2 * S
        cslot[fk * SLOTS : fk * SLOTS + HALF, :] = crow[fk // 2, at : at + HALF, :]
        cslot[fk * SLOTS + ROWS : fk * SLOTS + ROWS + S - HALF, :] = crow[fk // 2, at + HALF : at + S, :]
    wide[...] = dot_twice(cslot[...], spread[...])
    for k in range(8):
        k2, kk = k // 4, k % 4
        slabs = []
        for f in range(6):
            fine = jnp.concatenate(
                [got[2 * k, f * ROWS : (f + 1) * ROWS, :], got[2 * k + 1, f * ROWS : (f + 1) * ROWS, :]], 0
            )
            at = (f * 2 + k2) * SLOTS
            slabs.append(jnp.where(source[0, f] >= 0, fine, wide[at : at + SLOTS, 128 * kk : 128 * kk + 128]))
        for side in range(2):
            xs[side, :, 128 * k : 128 * k + 128] = slabs[side]
        for q, v in enumerate(swap_blocks(slabs[2:])):
            edge[pl.ds(4 * k + q, SLOTS, stride=32), :] = v
    copies[1].wait()
    copies[2].wait()
    kap = conduct[0]
    for side in range(2):
        xs[side] = xs[side] * kap[31 * side : 31 * side + 1]
    done = []
    for i, (lo, hi) in enumerate(CHUNKS):
        ghost = dot_twice(edge[slot(lo) * 32 : (slot(lo) + hi - lo) * 32, :], place[...])
        copies[3 + i].wait()
        for s in range(lo, hi):
            out[0, s] = inner[0, s] + rate[s] * (kap * ghost[(s - lo) * 32 : (s - lo + 1) * 32])
            for side in range(2):
                at = slice(31 * side, 31 * side + 1)
                out[0, s, at, :] = out[0, s, at, :] + rate[s] * xs[side, slot(s) : slot(s) + 1, :]
        c = pltpu.make_async_copy(out.at[:, lo:hi], out_hbm.at[:, lo:hi], sems.at[8 + i])
        c.start()
        done.append(c)
    kept.wait()
    for c in done:
        c.wait()


SPECS = {
    "v": pl.BlockSpec(memory_space=pltpu.VMEM),
    "s": pl.BlockSpec(memory_space=pltpu.SMEM),
    "a": pl.BlockSpec(memory_space=pl.ANY),
}


def call(kernel, ins, outs, spec, scratch, args, limit, copies=0, flops=int(1e9), alias={}):
    shapes = [jax.ShapeDtypeStruct(o, jnp.int32 if c == "s" else F32) for o, c in zip(outs, spec)]
    moved = sum(a.size * a.dtype.itemsize for a in args) + sum(4 * int(np.prod(o)) for o in outs)
    scratch = [x if not isinstance(x, tuple) else pltpu.VMEM(x, F32) for x in scratch]
    return pl.pallas_call(
        kernel,
        out_shape=shapes if len(outs) > 1 else shapes[0],
        in_specs=[SPECS[c] for c in ins],
        out_specs=[SPECS[c] for c in spec] if len(outs) > 1 else SPECS[spec],
        scratch_shapes=scratch + ([pltpu.SemaphoreType.DMA((copies,))] if copies else []),
        input_output_aliases=alias,
        compiler_params=pltpu.CompilerParams(vmem_limit_bytes=limit << 20),
        cost_estimate=pl.CostEstimate(flops=flops, bytes_accessed=moved, transcendentals=0),
        name=kernel.__name__.removesuffix("_kernel"),
    )(*args)


def shifted(block, distance):
    devices = range(lax.axis_size("sfc"))
    return lax.ppermute(block, "sfc", [(i, i + distance) for i in devices if i + distance in devices])


def exchange(block):
    return lax.all_to_all(block, "node", 0, 0, tiled=True)


def gathered(note, packed, first, second):
    me = lax.axis_index("node")
    parents = note[:, 6]
    parent = parents[me]
    ring = [(i, (i + 1) % PIECES) for i in range(PIECES)]
    size = 6 * FACE

    def faces_step(i, held):
        faces, ghost = held
        owner = (me - i) % PIECES
        mine = lax.dynamic_slice(faces, (parent % 8 * size, 0), (size, 128))
        ghost = jnp.where(parent // 8 == owner, mine, ghost)
        return lax.ppermute(faces, "node", ring), ghost

    _, ghost = lax.fori_loop(0, PIECES, faces_step, (packed[: 8 * size], jnp.zeros((size, 128), F32)))

    def flux_step(i, held):
        flux, rows = held
        box = (me - i) % PIECES
        at = (parents[box] % 8 * size, 0)
        added = lax.dynamic_slice(rows, at, (size, 128)) + flux
        return lax.ppermute(flux, "node", ring), jnp.where(parents[box] // 8 == me, lax.dynamic_update_slice(rows, added, at), rows)

    flux = first.reshape(size, 128) - second.reshape(size, 128) * ghost
    _, rows = lax.fori_loop(0, PIECES, flux_step, (flux, jnp.zeros((8 * size, 128), F32)))
    return ghost.reshape(6, FACE, 128), rows


def local(fine_state, conduct, spec_rate, reaction, coarse_state, ghost_source, parent_box):
    pick = jnp.asarray(pick_fine(), BF16)
    place = jnp.asarray(np.tile(pick_fine().T, (2, 1)), BF16)
    mean = jnp.asarray(average(), BF16)
    spread = jnp.asarray(np.tile(4 * average().T, (2, 1)), BF16)
    box = (1, S, B, AREA)
    fine, weighted = call(
        pack_fine_kernel,
        "aaaaa",
        [(PIECES, FINE, 128), (12 * SLOTS, 512)],
        "aa",
        [
            pltpu.SMEM((1, 6), jnp.int32), pltpu.SMEM((1,), jnp.int32), box, (1, B, AREA),
            pltpu.VMEM((AREA, 128), BF16), (PIECES, FINE, 128), (12 * SLOTS, 512), (SLOTS * 32, 128), (2, SLOTS, AREA),
        ],
        (ghost_source, parent_box, fine_state, conduct, pick),
        58,
        17,
    )
    own = exchange(fine)
    packed, first, second = call(
        pack_coarse_kernel,
        "aaaaaaa",
        [(48 * FACE + PIECES * MEANS, 128), (6, FACE, 128), (6, FACE, 128)],
        "aaa",
        [
            pltpu.SMEM((S,), F32), pltpu.SMEM((1, 6), jnp.int32), box, (12 * SLOTS, 512),
            pltpu.VMEM((AREA, 256), BF16), pltpu.VMEM((256, 256), BF16), pltpu.VMEM((512, 128), BF16),
            (2, S * 32, 128), (4 * SLOTS, AREA), (48 * FACE + PIECES * MEANS, 128), (6, FACE, 128), (6, FACE, 128),
        ],
        (spec_rate, ghost_source, coarse_state, weighted, jnp.asarray(pick_coarse(), BF16), jnp.asarray(split_octants(), BF16), mean),
        58,
        13,
    )
    note = own[:, 11, :8].astype(jnp.int32)
    coarse, listed = call(
        choose_kernel,
        "sv",
        [(PIECES, LIST + MEANS, 128), (CAP + 1,)],
        "as",
        [(PIECES, LIST + MEANS, 128), pltpu.SMEM((1,), jnp.int32)],
        (note, packed),
        24,
        1,
    )
    before, after = shifted(own, 1), shifted(own, -1)
    grouped = exchange(coarse)
    chosen, over = call(
        relay_kernel,
        "ssvvvv",
        [(PIECES, FINE + LIST, 128), (1,)],
        "as",
        [
            (PIECES, FINE + LIST, 128), (3 * 96, ROWS, 128), (PIECES * CAP, PART, 128), (PIECES * CAP + 1, PART, 128),
            pltpu.SMEM((PIECES,), jnp.int32),
        ],
        (note, spec_rate, before, own, after, grouped),
        24,
        1,
    )
    mine = exchange(chosen)
    inner = call(inner_kernel, "svvva", [box], "v", [(7, B, AREA)], (spec_rate, fine_state, conduct, reaction, chosen), 24)
    ghost, rows = lax.cond(
        over[0] > 0,
        gathered,
        lambda note, packed, first, second: (first, packed[: 48 * FACE]),
        note, packed, first, second,
    )
    tendency, register = call(
        outer_kernel,
        "ssssvaaaaaa",
        [box, (1, S, 48, 256)],
        "aa",
        [
            box, (1, B, AREA), pltpu.VMEM((256, 512), BF16), pltpu.VMEM((256, AREA), BF16), box, (1, S, 48, 256),
            (6, FACE, 128), (12 * SLOTS, 128), (12 * SLOTS, 512), (2, SLOTS, AREA), (SLOTS * 32, 128), (49 * FACE, 128), (CAP, FACE, 128),
        ],
        (spec_rate, ghost_source, listed, over, mine, inner, conduct, spread, place, ghost, rows),
        58,
        14,
    )
    return tendency, register.transpose(0, 2, 1, 3)


def solution(mesh):
    box = P(("sfc", "node"))
    return jax.shard_map(
        local,
        mesh=mesh,
        in_specs=(box, box, P(), P(), box, box, box),
        out_specs=(box, box),
        check_vma=False,
    )
```

time: 87.7 us -> 80.5 us (0.918); the launches traced: 86.2 us -> 80 us
  blocking collectives: 30.1 us -> 16.7 us
  Pallas kernels: 24.2 us -> 28.8 us
  starting transfers between devices: 15.2 us -> 16.8 us
  local copies, waits for them, and re-layouts: 3.69 us -> 4.89 us
  waiting for transfers between devices: 11.6 us -> 10.5 us
    all_to_all x1, blocking collectives: 30.1 us -> 16.7 us  [exchange(): return lax.all_to_all(block, 'node', 0, 0, tiled=True)]
    pallas_call x5 -> x6, Pallas kernels: 24.2 us -> 28.8 us  [call(): pl.pallas_call(kernel, out_shape=shapes if len(outs) > 1 else shapes[0],...]
    slice x0 -> x1, local copies, waits for them, and re-layouts: none -> 2.6 us  [local(): packed[:48 * FACE]]
    unnamed x18 -> x12, local copies, waits for them, and re-layouts: 3.69 us -> 1.57 us
    ppermute x2, starting transfers between devices: 2.62 us -> 4.36 us  [shifted(): lax.ppermute(block, 'sfc', [(i, i + distance) for i in devices if i + dis...]
    all_to_all x2, waiting for transfers between devices: 11.6 us -> 10.5 us  [exchange(): return lax.all_to_all(block, 'node', 0, 0, tiled=True)]
  transfers between devices with their start and end apart: 4 -> 4, of which waited for: 2 -> 2; matrix products, arithmetic and copies ran while one was open for 0% -> 4% of each run, Pallas kernels for 15% -> 20%
where the time goes in v2:
time: 80.5 us; the launch traced here: 80 us
  Pallas kernels  28.8 us (36%)
  starting transfers between devices  16.8 us (21%)
  blocking collectives  16.7 us (21%)
  waiting for transfers between devices  10.5 us (13%)
  local copies, waits for them, and re-layouts  4.89 us (6%)
  between operations  2.22 us (3%)
    pallas_call x6, Pallas kernels, call(): pl.pallas_call(kernel, out_shape=shapes if len(outs) > 1 else shapes[0],...  28.8 us
    all_to_all x1, blocking collectives, exchange(): return lax.all_to_all(block, 'node', 0, 0, tiled=True)  16.7 us
    all_to_all x2, starting transfers between devices, exchange(): return lax.all_to_all(block, 'node', 0, 0, tiled=True)  12.5 us
    all_to_all x2, waiting for transfers between devices, exchange(): return lax.all_to_all(block, 'node', 0, 0, tiled=True)  10.5 us
    ppermute x2, starting transfers between devices, shifted(): lax.ppermute(block, 'sfc', [(i, i + distance) for i in devices if i + dis...  4.36 us
    slice x1, local copies, waits for them, and re-layouts, local(): packed[:48 * FACE]  2.6 us
  transfers between devices with their start and end apart: 4, of which 2 were waited for; matrix products, arithmetic and copies ran while one was open for 4% of the time, Pallas kernels for 20%

profile of v2, /device:TPU:0, one launch (start us, length us, event | category | flops | bytes accessed | tf_op | source)
XLA Modules:
  0.0 80.0 jit_solution(6120389589463759393)
XLA Ops:
  1.3 4.1 %pack_fine.1 = (f32[16,72,128]{2,1,0:T(8,128)}, f32[288,512]{1,0:T(8,128)}) custom-call(s32[1,6]{1,0:T(1,128)} %source.1, s32[1]{0:T(128)S(6)} %copy.45.parent_in, f32[1,21,32,1024]{3,2,1,0:T(8,128)} %state.1, f32[1,32,1024]{2,1,0:T(8,128)} %conduct_in.3, bf16[1024,128]{1,0:T(8,128)(2,1)} %constant.256.clone.pick_in), custom_call_target="tpu_custom_call" | custom-call | flops 1000000000 | bytes 4325404 | tf_op jit(solution)/shard_map/pack_fine/pallas_call | solution.py:455
  5.4 8.1 %all-to-all-start = ((f32[16,72,128]{2,1,0:T(8,128)}), f32[16,72,128]{2,1,0:T(8,128)S(1)}, u32[]{:S(2)}, u32[]{:S(2)}) async-start(f32[16,72,128]{2,1,0:T(8,128)} %get-tuple-element.513), calls=%async_computation | async-start | bytes 1179648 | tf_op jit(solution)/shard_map/all_to_all | solution.py:474
  13.5 6.5 %pack_coarse.1 = (f32[2688,128]{1,0:T(8,128)}, f32[6,48,128]{2,1,0:T(8,128)S(1)}, f32[6,48,128]{2,1,0:T(8,128)S(1)}) custom-call(f32[21]{0:T(128)} %rate.5, s32[1,6]{1,0:T(1,128)} %source.1, f32[1,21,32,1024]{3,2,1,0:T(8,128)} %coarse_in.1, f32[288,512]{1,0:T(8,128)} %get-tuple-element.514.weighted_in, bf16[1024,256]{1,0:T(8,128)(2,1)} %constant.260.clone.pick_in, ...), custom_call_target="tpu_custom_call" | custom-call | flops 1000000000 | bytes 5800044 | tf_op jit(solution)/shard_map/pack_coarse/pallas_call | solution.py:455
  20.0 5.7 %all-to-all-done.own = f32[16,72,128]{2,1,0:T(8,128)S(1)} async-done(((f32[16,72,128]{2,1,0:T(8,128)}), f32[16,72,128]{2,1,0:T(8,128)S(1)}, u32[]{:S(2)}, u32[]{:S(2)}) %all-to-all-start) | async-done | bytes 589856 | tf_op jit(solution)/shard_map/all_to_all | solution.py:474
  25.7 1.3 %collective-permute-start.3 = (f32[16,72,128]{2,1,0:T(8,128)S(1)}, f32[16,72,128]{2,1,0:T(8,128)S(1)}, u32[]{:S(2)}, u32[]{:S(2)}) collective-permute-start(f32[16,72,128]{2,1,0:T(8,128)S(1)} %all-to-all-done.own), channel_id=1, source_target_pairs={{16,0},{32,16},{48,32},{64,48},{80,64},{96,80},{112,96},{17,1},{33... | collective-permute-start | bytes 1769480 | tf_op jit(solution)/shard_map/ppermute | solution.py:470
  27.0 3.1 %collective-permute-start.2 = (f32[16,72,128]{2,1,0:T(8,128)S(1)}, f32[16,72,128]{2,1,0:T(8,128)S(1)}, u32[]{:S(2)}, u32[]{:S(2)}) collective-permute-start(f32[16,72,128]{2,1,0:T(8,128)S(1)} %all-to-all-done.own), channel_id=1, source_target_pairs={{0,16},{16,32},{32,48},{48,64},{64,80},{80,96},{96,112},{1,17},{17... | collective-permute-start | bytes 1769480 | tf_op jit(solution)/shard_map/ppermute | solution.py:470
  30.1 2.6 %choose.1 = (f32[16,72,128]{2,1,0:T(8,128)S(1)}, s32[17]{0:T(128)S(1)}) custom-call(s32[16,8]{1,0:T(8,128)S(1)} %bitcast.19, f32[2688,128]{1,0:T(8,128)} %get-tuple-element.515.packed), custom_call_target="tpu_custom_call" | custom-call | flops 1000000000 | bytes 1966660 | tf_op jit(solution)/shard_map/choose/pallas_call | solution.py:455
  32.7 0.0 copy-start.5
  32.7 0.0 copy-start.4
  32.7 16.7 %all_to_all.15.got = f32[16,72,128]{2,1,0:T(8,128)S(1)} all-to-all(f32[16,72,128]{2,1,0:T(8,128)S(1)} %get-tuple-element.517), channel_id=1, replica_groups=mesh['sfc'=8,'node'=16] {'node'}, dimensions={0} | all-to-all | bytes 1179648 | tf_op jit(solution)/shard_map/all_to_all | solution.py:474
  49.4 0.0 collective-permute-done.3.after
  49.4 0.0 collective-permute-done.2.before
  49.4 0.0 copy-done.4
  49.4 3.2 %relay.1 = (f32[16,120,128]{2,1,0:T(8,128)}, s32[1]{0:T(128)}) custom-call(s32[16,8]{1,0:T(8,128)S(1)} %bitcast.20, f32[21]{0:T(128)S(1)} %copy-done.4, f32[16,72,128]{2,1,0:T(8,128)S(1)} %collective-permute-done.2.before, f32[16,72,128]{2,1,0:T(8,128)S(1)} %all-to-all-done.own, f32[16,72,128]{2,1,0:T(8,128)S(1)} %collective-permute-done.3.after, ...), custom_call_target="tpu_custom_call" | custom-call | flops 1000000000 | bytes 3342936 | tf_op jit(solution)/shard_map/relay/pallas_call | solution.py:455
  52.7 0.0 copy-done.5
  52.7 4.3 %all-to-all-start.2 = ((f32[16,120,128]{2,1,0:T(8,128)}), f32[16,120,128]{2,1,0:T(8,128)}, u32[]{:S(2)}, u32[]{:S(2)}) async-start(f32[16,120,128]{2,1,0:T(8,128)} %get-tuple-element.519.later), calls=%async_computation.2 | async-start | bytes 1966080 | tf_op jit(solution)/shard_map/all_to_all | solution.py:474
  57.0 0.1 copy.18
  57.7 0.0 copy-start.1
  57.7 0.0 copy-start.2
  57.7 0.0 copy-start.3
  57.8 3.3 %conditional.1 = (f32[6,48,128]{2,1,0:T(8,128)}, f32[2304,128]{1,0:T(8,128)}) conditional(s32[]{:T(128)} %bitcast.10, (f32[2688,128]{1,0:T(8,128)}, f32[6,48,128]{2,1,0:T(8,128)S(1)}) %tuple.69, (f32[2688,128]{1,0:T(8,128)}, s32[16,8]{0,1:T(8,128)S(1)}, f32[6,48,128]{2,1,0:T(8,128)S(1)}, f32[6,48,128]{2,1,0:T(8,128)S(1)}) %tuple.101), branch_computations={%region_0.0_spmd, %region_1.6_spmd} | conditional | flops 221269 | bytes 12977736 | solution.py:567
  57.8 0.7 copy.41
  58.4 2.6 %slice.8 = f32[2304,128]{1,0:T(8,128)} slice(f32[2688,128]{1,0:T(8,128)} %get-tuple-element.478), slice={[0:2304], [0:128]} | slice | bytes 2359296 | tf_op jit(solution)/shard_map/cond/branch_0_fun/slice | solution.py:570
  61.0 0.0 copy-done.1
  61.0 0.0 copy-done.2
  61.0 0.0 copy-done.3
  61.0 6.6 %inner.1.inner_in = f32[1,21,32,1024]{3,2,1,0:T(8,128)S(1)} custom-call(f32[21]{0:T(128)S(1)} %copy-done.4, f32[1,21,32,1024]{3,2,1,0:T(8,128)S(1)} %copy-done.1, f32[1,32,1024]{2,1,0:T(8,128)S(1)} %copy-done.2, f32[21,21]{1,0:T(8,128)S(1)} %copy-done.3, f32[16,120,128]{2,1,0:T(8,128)} %get-tuple-element.519.later), custom_call_target="tpu_custom_call" | custom-call | flops 1000000000 | bytes 6620984 | tf_op jit(solution)/shard_map/inner/pallas_call | solution.py:455
  67.6 0.0 copy-start
  67.6 1.5 %copy-done = f32[1,21,32,1024]{3,2,1,0:T(8,128)} copy-done((f32[1,21,32,1024]{3,2,1,0:T(8,128)}, f32[1,21,32,1024]{3,2,1,0:T(8,128)S(1)}, u32[]{:S(2)}) %copy-start) | copy-done | bytes 2752536
  69.2 4.8 %all-to-all-done.2.got = f32[16,120,128]{2,1,0:T(8,128)} async-done(((f32[16,120,128]{2,1,0:T(8,128)}), f32[16,120,128]{2,1,0:T(8,128)}, u32[]{:S(2)}, u32[]{:S(2)}) %all-to-all-start.2) | async-done | bytes 983072 | tf_op jit(solution)/shard_map/all_to_all | solution.py:474
  74.0 5.9 %outer.1 = (f32[1,21,32,1024]{3,2,1,0:T(8,128)}, f32[1,21,48,256]{3,2,1,0:T(8,128)}) custom-call(f32[21]{0:T(128)} %rate.5, s32[1,6]{1,0:T(1,128)} %source.1, s32[17]{0:T(128)} %copy-done.5, s32[1]{0:T(128)} %get-tuple-element.518.over, f32[16,120,128]{2,1,0:T(8,128)} %all-to-all-done.2.got, f32[1,21,32,1024]{3,2,1,0:T(8,128)} %copy-done, ...), custom_call_target="tpu_custom_call" | custom-call | flops 1000000000 | bytes 9765044 | tf_op jit(solution)/shard_map/outer/pallas_call | solution.py:455
  (1 shorter events, 0.0 us)
Async XLA Ops:
  5.4 20.4 %all-to-all-start = ((f32[16,72,128]{2,1,0:T(8,128)}), f32[16,72,128]{2,1,0:T(8,128)S(1)}, u32[]{:S(2)}, u32[]{:S(2)}) async-start(f32[16,72,128]{2,1,0:T(8,128)} %get-tuple-element.513), calls=%async_computation | async-start | bytes 1179648 | tf_op jit(solution)/shard_map/all_to_all | solution.py:474
  25.7 23.7 %collective-permute-start.3 = (f32[16,72,128]{2,1,0:T(8,128)S(1)}, f32[16,72,128]{2,1,0:T(8,128)S(1)}, u32[]{:S(2)}, u32[]{:S(2)}) collective-permute-start(f32[16,72,128]{2,1,0:T(8,128)S(1)} %all-to-all-done.own), channel_id=1, source_target_pairs={{16,0},{32,16},{48,32},{64,48},{80,64},{96,80},{112,96},{17,1},{33... | collective-permute-start | bytes 1769480 | tf_op jit(solution)/shard_map/ppermute | solution.py:470
  27.0 22.4 %collective-permute-start.2 = (f32[16,72,128]{2,1,0:T(8,128)S(1)}, f32[16,72,128]{2,1,0:T(8,128)S(1)}, u32[]{:S(2)}, u32[]{:S(2)}) collective-permute-start(f32[16,72,128]{2,1,0:T(8,128)S(1)} %all-to-all-done.own), channel_id=1, source_target_pairs={{0,16},{16,32},{32,48},{48,64},{64,80},{80,96},{96,112},{1,17},{17... | collective-permute-start | bytes 1769480 | tf_op jit(solution)/shard_map/ppermute | solution.py:470
  32.7 19.9 %copy-start.5 = (s32[17]{0:T(128)}, s32[17]{0:T(128)S(1)}, u32[]{:S(2)}) copy-start(s32[17]{0:T(128)S(1)} %get-tuple-element.516.listed) | copy-start | bytes 208
  32.7 16.7 %copy-start.4 = (f32[21]{0:T(128)S(1)}, f32[21]{0:T(128)}, u32[]{:S(2)}) copy-start(f32[21]{0:T(128)} %rate.5) | copy-start | bytes 256
  52.7 21.4 %all-to-all-start.2 = ((f32[16,120,128]{2,1,0:T(8,128)}), f32[16,120,128]{2,1,0:T(8,128)}, u32[]{:S(2)}, u32[]{:S(2)}) async-start(f32[16,120,128]{2,1,0:T(8,128)} %get-tuple-element.519.later), calls=%async_computation.2 | async-start | bytes 1966080 | tf_op jit(solution)/shard_map/all_to_all | solution.py:474
  57.7 3.3 %copy-start.1 = (f32[1,21,32,1024]{3,2,1,0:T(8,128)S(1)}, f32[1,21,32,1024]{3,2,1,0:T(8,128)}, u32[]{:S(2)}) copy-start(f32[1,21,32,1024]{3,2,1,0:T(8,128)} %state.1) | copy-start | bytes 8257540
  57.7 3.3 %copy-start.2 = (f32[1,32,1024]{2,1,0:T(8,128)S(1)}, f32[1,32,1024]{2,1,0:T(8,128)}, u32[]{:S(2)}) copy-start(f32[1,32,1024]{2,1,0:T(8,128)} %conduct_in.3) | copy-start | bytes 393220
  57.7 3.3 %copy-start.3 = (f32[21,21]{1,0:T(8,128)S(1)}, f32[21,21]{1,0:T(8,128)}, u32[]{:S(2)}) copy-start(f32[21,21]{1,0:T(8,128)} %react.1) | copy-start | bytes 5296
  67.6 1.5 %copy-start = (f32[1,21,32,1024]{3,2,1,0:T(8,128)}, f32[1,21,32,1024]{3,2,1,0:T(8,128)S(1)}, u32[]{:S(2)}) copy-start(f32[1,21,32,1024]{3,2,1,0:T(8,128)S(1)} %inner.1.inner_in) | copy-start | bytes 8257540

commit v3 on v2

--- a/solution.py
+++ b/solution.py
@@ -309,8 +309,9 @@
         got = jnp.dot(react_hi, hi, preferred_element_type=F32)
         got += jnp.dot(react_hi, lo, preferred_element_type=F32)
         got += jnp.dot(react_lo, hi, preferred_element_type=F32)
-        out[0, :, g * 8 : g * 8 + 8, :] = got.reshape(S, 8, AREA)
-
+        out[0, :S, g * 8 : g * 8 + 8, :] = got.reshape(S, 8, AREA)
+
+    out[0, S] = kap
     def species(s, carry):
         u = state[0, s]
         acc = -coef[6] * u
@@ -322,7 +323,7 @@
     lax.fori_loop(0, S, species, 0)
 
 
-def relay_kernel(note, rate, before, own, after, got, out_hbm, over, out, table, listed, fluxes, seen, sems):
+def relay_kernel(note, chosen, rate, before, own, after, got, out_hbm, plan, out, table, listed, fluxes, seen, sems):
     for c in range(PIECES):
         seen[c] = 0
     j = lax.axis_index("node")
@@ -356,24 +357,40 @@
     most = seen[0]
     for c in range(1, PIECES):
         most = jnp.maximum(most, seen[c])
-    over[0] = (most > CAP).astype(jnp.int32)
+    plan[0] = (most > CAP).astype(jnp.int32)
+    for i in range(CAP):
+        plan[1 + i] = chosen[i]
+    for f in range(6):
+        plan[1 + CAP + f] = note[j, f]
+    slots = pltpu.make_async_copy(out.at[:, :FINE], out_hbm.at[:, :FINE], sems.at[0])
+    slots.start()
     for c in range(PIECES):
         for i in range(CAP):
             out[c, FINE + PART * i : FINE + PART * i + PART, :] = fluxes[c * CAP + i, :PART, :]
-    sent = pltpu.make_async_copy(out, out_hbm, sems.at[0])
+    sent = pltpu.make_async_copy(out.at[:, FINE:], out_hbm.at[:, FINE:], sems.at[1])
     sent.start()
+    slots.wait()
     sent.wait()
 
 
+def spread_matrix():
+    r = lax.broadcasted_iota(jnp.int32, (256, 512), 0) % 128
+    c = lax.broadcasted_iota(jnp.int32, (256, 512), 1)
+    return jnp.logical_and(r // 16 == c // 64, r % 16 == c % 32 // 2).astype(F32).astype(BF16)
+
+
+def place_matrix():
+    r = lax.broadcasted_iota(jnp.int32, (256, AREA), 0) % 128
+    c = lax.broadcasted_iota(jnp.int32, (256, AREA), 1)
+    y, z, f, b = c // 32, c % 32, r // 32, r % 32
+    at, along = jnp.where(f < 2, y, z), jnp.where(f < 2, z, y)
+    return jnp.logical_and(at == (f % 2) * 31, along == b).astype(F32).astype(BF16)
+
+
 def outer_kernel(
-    rate, source, listed, over, got, inner_in, conduct_in, spread_in, place_in, ghost_in, rows_in, out_hbm, reg_hbm,
-    inner, conduct, spread, place, out, reg, crow, cslot, wide, xs, edge, table, held, sems,
+    rate, plan, got, inner, ghost_in, rows_in, out_hbm, reg_hbm,
+    out, reg, crow, cslot, wide, xs, edge, table, held, sems,
 ):
-    copies = begin(
-        sems,
-        [(spread_in, spread), (place_in, place), (conduct_in, conduct)]
-        + [(inner_in.at[:, lo:hi], inner.at[:, lo:hi]) for lo, hi in CHUNKS],
-    )
     table[...] = jnp.zeros_like(table)
     for i in range(CAP):
         held[i, 2 * S :, :] = jnp.zeros((FACE - 2 * S, 128), F32)
@@ -384,10 +401,10 @@
         for i in range(CAP):
             held[i, at, :] = got[j, FINE + PART * i : FINE + PART * i + PART, :]
     for i in range(CAP):
-        face = pl.ds(pl.multiple_of(listed[i] * FACE, 8), FACE)
+        face = pl.ds(pl.multiple_of(plan[1 + i] * FACE, 8), FACE)
         table[face, :] = table[face, :] + held[i]
 
-    @pl.when(over[0] > 0)
+    @pl.when(plan[0] > 0)
     def _():
         for src, dst, sem in ((ghost_in, crow, sems.at[12]), (rows_in, table.at[: 48 * FACE], sems.at[13])):
             c = pltpu.make_async_copy(src, dst, sem)
@@ -399,13 +416,12 @@
             reg[0, s, :, k2 * 128 : k2 * 128 + 128] = table[pl.ds(k2 * S + s, 48, stride=FACE), :]
     kept = pltpu.make_async_copy(reg, reg_hbm, sems.at[7])
     kept.start()
-    copies[0].wait()
     cslot[...] = jnp.zeros_like(cslot)
     for fk in range(12):
         at = fk % 2 * S
         cslot[fk * SLOTS : fk * SLOTS + HALF, :] = crow[fk // 2, at : at + HALF, :]
         cslot[fk * SLOTS + ROWS : fk * SLOTS + ROWS + S - HALF, :] = crow[fk // 2, at + HALF : at + S, :]
-    wide[...] = dot_twice(cslot[...], spread[...])
+    wide[...] = dot_twice(cslot[...], spread_matrix())
     for k in range(8):
         k2, kk = k // 4, k % 4
         slabs = []
@@ -414,20 +430,18 @@
                 [got[2 * k, f * ROWS : (f + 1) * ROWS, :], got[2 * k + 1, f * ROWS : (f + 1) * ROWS, :]], 0
             )
             at = (f * 2 + k2) * SLOTS
-            slabs.append(jnp.where(source[0, f] >= 0, fine, wide[at : at + SLOTS, 128 * kk : 128 * kk + 128]))
+            slabs.append(jnp.where(plan[1 + CAP + f] >= 0, fine, wide[at : at + SLOTS, 128 * kk : 128 * kk + 128]))
         for side in range(2):
             xs[side, :, 128 * k : 128 * k + 128] = slabs[side]
         for q, v in enumerate(swap_blocks(slabs[2:])):
             edge[pl.ds(4 * k + q, SLOTS, stride=32), :] = v
-    copies[1].wait()
-    copies[2].wait()
-    kap = conduct[0]
+    kap = inner[0, S]
+    place = place_matrix()
     for side in range(2):
         xs[side] = xs[side] * kap[31 * side : 31 * side + 1]
     done = []
     for i, (lo, hi) in enumerate(CHUNKS):
-        ghost = dot_twice(edge[slot(lo) * 32 : (slot(lo) + hi - lo) * 32, :], place[...])
-        copies[3 + i].wait()
+        ghost = dot_twice(edge[slot(lo) * 32 : (slot(lo) + hi - lo) * 32, :], place)
         for s in range(lo, hi):
             out[0, s] = inner[0, s] + rate[s] * (kap * ghost[(s - lo) * 32 : (s - lo + 1) * 32])
             for side in range(2):
@@ -504,9 +518,7 @@
 
 def local(fine_state, conduct, spec_rate, reaction, coarse_state, ghost_source, parent_box):
     pick = jnp.asarray(pick_fine(), BF16)
-    place = jnp.asarray(np.tile(pick_fine().T, (2, 1)), BF16)
     mean = jnp.asarray(average(), BF16)
-    spread = jnp.asarray(np.tile(4 * average().T, (2, 1)), BF16)
     box = (1, S, B, AREA)
     fine, weighted = call(
         pack_fine_kernel,
@@ -549,38 +561,38 @@
     )
     before, after = shifted(own, 1), shifted(own, -1)
     grouped = exchange(coarse)
-    chosen, over = call(
+    chosen, plan = call(
         relay_kernel,
-        "ssvvvv",
-        [(PIECES, FINE + LIST, 128), (1,)],
+        "sssvvvv",
+        [(PIECES, FINE + LIST, 128), (1 + CAP + 6,)],
         "as",
         [
             (PIECES, FINE + LIST, 128), (3 * 96, ROWS, 128), (PIECES * CAP, PART, 128), (PIECES * CAP + 1, PART, 128),
             pltpu.SMEM((PIECES,), jnp.int32),
         ],
-        (note, spec_rate, before, own, after, grouped),
+        (note, listed, spec_rate, before, own, after, grouped),
         24,
-        1,
+        2,
     )
     mine = exchange(chosen)
-    inner = call(inner_kernel, "svvva", [box], "v", [(7, B, AREA)], (spec_rate, fine_state, conduct, reaction, chosen), 24)
+    inner = call(inner_kernel, "svvva", [(1, S + 1, B, AREA)], "v", [(7, B, AREA)], (spec_rate, fine_state, conduct, reaction, chosen), 24)
     ghost, rows = lax.cond(
-        over[0] > 0,
+        plan[0] > 0,
         gathered,
         lambda note, packed, first, second: (first, packed[: 48 * FACE]),
         note, packed, first, second,
     )
     tendency, register = call(
         outer_kernel,
-        "ssssvaaaaaa",
+        "ssvvaa",
         [box, (1, S, 48, 256)],
         "aa",
         [
-            box, (1, B, AREA), pltpu.VMEM((256, 512), BF16), pltpu.VMEM((256, AREA), BF16), box, (1, S, 48, 256),
+            box, (1, S, 48, 256),
             (6, FACE, 128), (12 * SLOTS, 128), (12 * SLOTS, 512), (2, SLOTS, AREA), (SLOTS * 32, 128), (49 * FACE, 128), (CAP, FACE, 128),
         ],
-        (spec_rate, ghost_source, listed, over, mine, inner, conduct, spread, place, ghost, rows),
-        58,
+        (spec_rate, plan, mine, inner, ghost, rows),
+        28,
         14,
     )
     return tendency, register.transpose(0, 2, 1, 3)

time: 80.5 us -> 78.7 us (0.978)
  waiting for transfers between devices: 10.5 us -> 13 us
  Pallas kernels: 28.8 us -> 26.4 us
  local copies, waits for them, and re-layouts: 4.89 us -> 3.63 us
    all_to_all x2, waiting for transfers between devices: 10.5 us -> 13 us  [exchange(): return lax.all_to_all(block, 'node', 0, 0, tiled=True)]
    pallas_call x6, Pallas kernels: 28.8 us -> 26.4 us  [call(): pl.pallas_call(kernel, out_shape=shapes if len(outs) > 1 else shapes[0],...]
    slice x1, local copies, waits for them, and re-layouts: 2.6 us -> 1.11 us  [local(): packed[:48 * FACE]]
    unnamed x12 -> x8, local copies, waits for them, and re-layouts: 1.57 us -> 1.79 us
  transfers between devices with their start and end apart: 4 -> 4, of which waited for: 2 -> 2; matrix products, arithmetic and copies ran while one was open for 4% -> 2% of each run, Pallas kernels for 20% -> 18%
where the time goes in v3:
time: 78.7 us; the launch traced here: 78.2 us
  Pallas kernels  26.4 us (34%)
  starting transfers between devices  16.8 us (21%)
  blocking collectives  16.7 us (21%)
  waiting for transfers between devices  13 us (17%)
  local copies, waits for them, and re-layouts  3.63 us (5%)
  between operations  1.59 us (2%)
    pallas_call x6, Pallas kernels, call(): pl.pallas_call(kernel, out_shape=shapes if len(outs) > 1 else shapes[0],...  26.4 us
    all_to_all x1, blocking collectives, exchange(): return lax.all_to_all(block, 'node', 0, 0, tiled=True)  16.7 us
    all_to_all x2, waiting for transfers between devices, exchange(): return lax.all_to_all(block, 'node', 0, 0, tiled=True)  13 us
    all_to_all x2, starting transfers between devices, exchange(): return lax.all_to_all(block, 'node', 0, 0, tiled=True)  12.5 us
    ppermute x2, starting transfers between devices, shifted(): lax.ppermute(block, 'sfc', [(i, i + distance) for i in devices if i + dis...  4.36 us
    unnamed x8, local copies, waits for them, and re-layouts  1.79 us
  transfers between devices with their start and end apart: 4, of which 2 were waited for; matrix products, arithmetic and copies ran while one was open for 2% of the time, Pallas kernels for 18%

profile of v3, /device:TPU:0, one launch (start us, length us, event | category | flops | bytes accessed | tf_op | source)
XLA Modules:
  0.0 78.2 jit_solution(15414178282370682408)
XLA Ops:
  1.3 4.1 %pack_fine.1 = (f32[16,72,128]{2,1,0:T(8,128)}, f32[288,512]{1,0:T(8,128)}) custom-call(s32[1,6]{1,0:T(1,128)} %source_in.3, s32[1]{0:T(128)S(6)} %copy.43.parent_in, f32[1,21,32,1024]{3,2,1,0:T(8,128)} %state.1, f32[1,32,1024]{2,1,0:T(8,128)} %conduct.1, bf16[1024,128]{1,0:T(8,128)(2,1)} %constant.252.clone.pick_in), custom_call_target="tpu_custom_call" | custom-call | flops 1000000000 | bytes 4325404 | tf_op jit(solution)/shard_map/pack_fine/pallas_call | solution.py:469
  5.3 8.1 %all-to-all-start = ((f32[16,72,128]{2,1,0:T(8,128)}), f32[16,72,128]{2,1,0:T(8,128)S(1)}, u32[]{:S(2)}, u32[]{:S(2)}) async-start(f32[16,72,128]{2,1,0:T(8,128)} %get-tuple-element.513), calls=%async_computation | async-start | bytes 1179648 | tf_op jit(solution)/shard_map/all_to_all | solution.py:488
  13.5 5.9 %pack_coarse.1 = (f32[2688,128]{1,0:T(8,128)S(1)}, f32[6,48,128]{2,1,0:T(8,128)S(1)}, f32[6,48,128]{2,1,0:T(8,128)S(1)}) custom-call(f32[21]{0:T(128)} %rate.5, s32[1,6]{1,0:T(1,128)} %source_in.3, f32[1,21,32,1024]{3,2,1,0:T(8,128)} %coarse_in.1, f32[288,512]{1,0:T(8,128)} %get-tuple-element.514.weighted_in, bf16[1024,256]{1,0:T(8,128)(2,1)} %constant.254.clone.pick_in, ...), custom_call_target="tpu_custom_call" | custom-call | flops 1000000000 | bytes 5800044 | tf_op jit(solution)/shard_map/pack_coarse/pallas_call | solution.py:469
  19.4 6.3 %all-to-all-done.own = f32[16,72,128]{2,1,0:T(8,128)S(1)} async-done(((f32[16,72,128]{2,1,0:T(8,128)}), f32[16,72,128]{2,1,0:T(8,128)S(1)}, u32[]{:S(2)}, u32[]{:S(2)}) %all-to-all-start) | async-done | bytes 589856 | tf_op jit(solution)/shard_map/all_to_all | solution.py:488
  25.7 1.3 %collective-permute-start.3 = (f32[16,72,128]{2,1,0:T(8,128)S(1)}, f32[16,72,128]{2,1,0:T(8,128)S(1)}, u32[]{:S(2)}, u32[]{:S(2)}) collective-permute-start(f32[16,72,128]{2,1,0:T(8,128)S(1)} %all-to-all-done.own), channel_id=1, source_target_pairs={{16,0},{32,16},{48,32},{64,48},{80,64},{96,80},{112,96},{17,1},{33... | collective-permute-start | bytes 1769480 | tf_op jit(solution)/shard_map/ppermute | solution.py:484
  27.0 3.1 %collective-permute-start.2 = (f32[16,72,128]{2,1,0:T(8,128)S(1)}, f32[16,72,128]{2,1,0:T(8,128)S(1)}, u32[]{:S(2)}, u32[]{:S(2)}) collective-permute-start(f32[16,72,128]{2,1,0:T(8,128)S(1)} %all-to-all-done.own), channel_id=1, source_target_pairs={{0,16},{16,32},{32,48},{48,64},{64,80},{80,96},{96,112},{1,17},{17... | collective-permute-start | bytes 1769480 | tf_op jit(solution)/shard_map/ppermute | solution.py:484
  30.1 1.9 %choose.1 = (f32[16,72,128]{2,1,0:T(8,128)S(1)}, s32[17]{0:T(128)S(1)}) custom-call(s32[16,8]{1,0:T(8,128)S(1)} %bitcast.20, f32[2688,128]{1,0:T(8,128)S(1)} %get-tuple-element.515.packed), custom_call_target="tpu_custom_call" | custom-call | flops 1000000000 | bytes 1966660 | tf_op jit(solution)/shard_map/choose/pallas_call | solution.py:469
  32.0 0.0 copy-start.3
  32.0 16.7 %all_to_all.15.got = f32[16,72,128]{2,1,0:T(8,128)S(1)} all-to-all(f32[16,72,128]{2,1,0:T(8,128)S(1)} %get-tuple-element.517), channel_id=1, replica_groups=mesh['sfc'=8,'node'=16] {'node'}, dimensions={0} | all-to-all | bytes 1179648 | tf_op jit(solution)/shard_map/all_to_all | solution.py:488
  48.7 0.0 collective-permute-done.3.after
  48.7 0.0 collective-permute-done.2.before
  48.7 0.0 copy-done.3
  48.7 3.2 %relay.1 = (f32[16,120,128]{2,1,0:T(8,128)}, s32[23]{0:T(128)S(1)}) custom-call(s32[16,8]{1,0:T(8,128)S(1)} %bitcast.21, s32[17]{0:T(128)S(1)} %get-tuple-element.516.chosen, f32[21]{0:T(128)S(1)} %copy-done.3, f32[16,72,128]{2,1,0:T(8,128)S(1)} %collective-permute-done.2.before, f32[16,72,128]{2,1,0:T(8,128)S(1)} %all-to-all-done.own, ...), custom_call_target="tpu_custom_call" | custom-call | flops 1000000000 | bytes 3343092 | tf_op jit(solution)/shard_map/relay/pallas_call | solution.py:469
  52.0 4.3 %all-to-all-start.2 = ((f32[16,120,128]{2,1,0:T(8,128)}), f32[16,120,128]{2,1,0:T(8,128)}, u32[]{:S(2)}, u32[]{:S(2)}) async-start(f32[16,120,128]{2,1,0:T(8,128)} %get-tuple-element.519.later), calls=%async_computation.2 | async-start | bytes 1966080 | tf_op jit(solution)/shard_map/all_to_all | solution.py:488
  56.3 0.1 copy.16
  56.4 0.0 copy-start.1
  56.4 0.0 copy-start.2
  56.5 1.8 %conditional.1 = (f32[6,48,128]{2,1,0:T(8,128)}, f32[2304,128]{1,0:T(8,128)}) conditional(s32[]{:T(128)} %bitcast.10, (f32[2688,128]{1,0:T(8,128)S(1)}, f32[6,48,128]{2,1,0:T(8,128)S(1)}) %tuple.69, (f32[2688,128]{1,0:T(8,128)S(1)}, s32[16,8]{0,1:T(8,128)S(1)}, f32[6,48,128]{2,1,0:T(8,128)S(1)}, f32[6,48,128]{2,1,0:T(8,128)S(1)}) %tuple.101), branch_computations={%region_0.0_spmd, %region_1.6_spmd} | conditional | flops 221269 | bytes 12977736 | solution.py:579
  56.5 0.7 copy.39
  57.1 1.1 %slice.10 = f32[2304,128]{1,0:T(8,128)} slice(f32[2688,128]{1,0:T(8,128)S(1)} %get-tuple-element.478), slice={[0:2304], [0:128]} | slice | bytes 2359296 | tf_op jit(solution)/shard_map/cond/branch_0_fun/slice | solution.py:582
  58.2 0.0 copy-done.1
  58.2 0.0 copy-done.2
  58.2 0.0 copy-start
  58.2 1.8 %copy-done = f32[1,21,32,1024]{3,2,1,0:T(8,128)S(1)} copy-done((f32[1,21,32,1024]{3,2,1,0:T(8,128)S(1)}, f32[1,21,32,1024]{3,2,1,0:T(8,128)}, u32[]{:S(2)}) %copy-start) | copy-done | bytes 2752536
  60.0 6.6 %inner.1 = f32[1,22,32,1024]{3,2,1,0:T(8,128)S(1)} custom-call(f32[21]{0:T(128)S(1)} %copy-done.3, f32[1,21,32,1024]{3,2,1,0:T(8,128)S(1)} %copy-done, f32[1,32,1024]{2,1,0:T(8,128)S(1)} %copy-done.1, f32[21,21]{1,0:T(8,128)S(1)} %copy-done.2, f32[16,120,128]{2,1,0:T(8,128)} %get-tuple-element.519.later), custom_call_target="tpu_custom_call" | custom-call | flops 1000000000 | bytes 6752056 | tf_op jit(solution)/shard_map/inner/pallas_call | solution.py:469
  66.6 6.7 %all-to-all-done.2.got = f32[16,120,128]{2,1,0:T(8,128)} async-done(((f32[16,120,128]{2,1,0:T(8,128)}), f32[16,120,128]{2,1,0:T(8,128)}, u32[]{:S(2)}, u32[]{:S(2)}) %all-to-all-start.2) | async-done | bytes 983072 | tf_op jit(solution)/shard_map/all_to_all | solution.py:488
  73.3 4.7 %outer.1 = (f32[1,21,32,1024]{3,2,1,0:T(8,128)}, f32[1,21,48,256]{3,2,1,0:T(8,128)}) custom-call(f32[21]{0:T(128)S(1)} %copy-done.3, s32[23]{0:T(128)S(1)} %get-tuple-element.518.plan, f32[16,120,128]{2,1,0:T(8,128)} %all-to-all-done.2.got, f32[1,22,32,1024]{3,2,1,0:T(8,128)S(1)} %inner.1, f32[6,48,128]{2,1,0:T(8,128)} %get-tuple-element.522.ghost_in, ...), custom_call_target="tpu_custom_call" | custom-call | flops 1000000000 | bytes 8978608 | tf_op jit(solution)/shard_map/outer/pallas_call | solution.py:469
  (1 shorter events, 0.0 us)
Async XLA Ops:
  5.3 20.4 %all-to-all-start = ((f32[16,72,128]{2,1,0:T(8,128)}), f32[16,72,128]{2,1,0:T(8,128)S(1)}, u32[]{:S(2)}, u32[]{:S(2)}) async-start(f32[16,72,128]{2,1,0:T(8,128)} %get-tuple-element.513), calls=%async_computation | async-start | bytes 1179648 | tf_op jit(solution)/shard_map/all_to_all | solution.py:488
  25.7 23.0 %collective-permute-start.3 = (f32[16,72,128]{2,1,0:T(8,128)S(1)}, f32[16,72,128]{2,1,0:T(8,128)S(1)}, u32[]{:S(2)}, u32[]{:S(2)}) collective-permute-start(f32[16,72,128]{2,1,0:T(8,128)S(1)} %all-to-all-done.own), channel_id=1, source_target_pairs={{16,0},{32,16},{48,32},{64,48},{80,64},{96,80},{112,96},{17,1},{33... | collective-permute-start | bytes 1769480 | tf_op jit(solution)/shard_map/ppermute | solution.py:484
  27.0 21.7 %collective-permute-start.2 = (f32[16,72,128]{2,1,0:T(8,128)S(1)}, f32[16,72,128]{2,1,0:T(8,128)S(1)}, u32[]{:S(2)}, u32[]{:S(2)}) collective-permute-start(f32[16,72,128]{2,1,0:T(8,128)S(1)} %all-to-all-done.own), channel_id=1, source_target_pairs={{0,16},{16,32},{32,48},{48,64},{64,80},{80,96},{96,112},{1,17},{17... | collective-permute-start | bytes 1769480 | tf_op jit(solution)/shard_map/ppermute | solution.py:484
  32.0 16.7 %copy-start.3 = (f32[21]{0:T(128)S(1)}, f32[21]{0:T(128)}, u32[]{:S(2)}) copy-start(f32[21]{0:T(128)} %rate.5) | copy-start | bytes 256
  52.0 21.4 %all-to-all-start.2 = ((f32[16,120,128]{2,1,0:T(8,128)}), f32[16,120,128]{2,1,0:T(8,128)}, u32[]{:S(2)}, u32[]{:S(2)}) async-start(f32[16,120,128]{2,1,0:T(8,128)} %get-tuple-element.519.later), calls=%async_computation.2 | async-start | bytes 1966080 | tf_op jit(solution)/shard_map/all_to_all | solution.py:488
  56.4 1.8 %copy-start.1 = (f32[1,32,1024]{2,1,0:T(8,128)S(1)}, f32[1,32,1024]{2,1,0:T(8,128)}, u32[]{:S(2)}) copy-start(f32[1,32,1024]{2,1,0:T(8,128)} %conduct.1) | copy-start | bytes 393220
  56.4 1.8 %copy-start.2 = (f32[21,21]{1,0:T(8,128)S(1)}, f32[21,21]{1,0:T(8,128)}, u32[]{:S(2)}) copy-start(f32[21,21]{1,0:T(8,128)} %react.1) | copy-start | bytes 5296
  58.2 1.8 %copy-start = (f32[1,21,32,1024]{3,2,1,0:T(8,128)S(1)}, f32[1,21,32,1024]{3,2,1,0:T(8,128)}, u32[]{:S(2)}) copy-start(f32[1,21,32,1024]{3,2,1,0:T(8,128)} %state.1) | copy-start | bytes 8257540

commit v4 on v3

--- a/solution.py
+++ b/solution.py
@@ -374,17 +374,19 @@
 
 
 def spread_matrix():
-    r = lax.broadcasted_iota(jnp.int32, (256, 512), 0) % 128
-    c = lax.broadcasted_iota(jnp.int32, (256, 512), 1)
-    return jnp.logical_and(r // 16 == c // 64, r % 16 == c % 32 // 2).astype(F32).astype(BF16)
+    r = lax.broadcasted_iota(jnp.int32, (128, 512), 0)
+    c = lax.broadcasted_iota(jnp.int32, (128, 512), 1)
+    m = jnp.logical_and(r // 16 == c // 64, r % 16 == c % 32 // 2).astype(F32).astype(BF16)
+    return jnp.concatenate([m, m], 0)
 
 
 def place_matrix():
-    r = lax.broadcasted_iota(jnp.int32, (256, AREA), 0) % 128
-    c = lax.broadcasted_iota(jnp.int32, (256, AREA), 1)
+    r = lax.broadcasted_iota(jnp.int32, (128, AREA), 0)
+    c = lax.broadcasted_iota(jnp.int32, (128, AREA), 1)
     y, z, f, b = c // 32, c % 32, r // 32, r % 32
     at, along = jnp.where(f < 2, y, z), jnp.where(f < 2, z, y)
-    return jnp.logical_and(at == (f % 2) * 31, along == b).astype(F32).astype(BF16)
+    m = jnp.logical_and(at == (f % 2) * 31, along == b).astype(F32).astype(BF16)
+    return jnp.concatenate([m, m], 0)
 
 
 def outer_kernel(

time: 78.7 us -> 78.6 us (level)
  no operation moved by 1% of the time
where the time goes in v4:
time: 78.6 us; the launch traced here: 78.1 us
  Pallas kernels  26.4 us (34%)
  starting transfers between devices  16.8 us (21%)
  blocking collectives  16.7 us (21%)
  waiting for transfers between devices  13 us (17%)
  local copies, waits for them, and re-layouts  3.63 us (5%)
  between operations  1.59 us (2%)
    pallas_call x6, Pallas kernels, call(): pl.pallas_call(kernel, out_shape=shapes if len(outs) > 1 else shapes[0],...  26.4 us
    all_to_all x1, blocking collectives, exchange(): return lax.all_to_all(block, 'node', 0, 0, tiled=True)  16.7 us
    all_to_all x2, waiting for transfers between devices, exchange(): return lax.all_to_all(block, 'node', 0, 0, tiled=True)  13 us
    all_to_all x2, starting transfers between devices, exchange(): return lax.all_to_all(block, 'node', 0, 0, tiled=True)  12.5 us
    ppermute x2, starting transfers between devices, shifted(): lax.ppermute(block, 'sfc', [(i, i + distance) for i in devices if i + dis...  4.36 us
    unnamed x8, local copies, waits for them, and re-layouts  1.79 us
  transfers between devices with their start and end apart: 4, of which 2 were waited for; matrix products, arithmetic and copies ran while one was open for 2% of the time, Pallas kernels for 18%

profile of v4, /device:TPU:0, one launch (start us, length us, event | category | flops | bytes accessed | tf_op | source)
XLA Modules:
  0.0 78.1 jit_solution(3618339605771643446)
XLA Ops:
  1.3 4.1 %pack_fine.1 = (f32[16,72,128]{2,1,0:T(8,128)}, f32[288,512]{1,0:T(8,128)}) custom-call(s32[1,6]{1,0:T(1,128)} %source_in.3, s32[1]{0:T(128)S(6)} %copy.43.parent_in, f32[1,21,32,1024]{3,2,1,0:T(8,128)} %state.1, f32[1,32,1024]{2,1,0:T(8,128)} %conduct.1, bf16[1024,128]{1,0:T(8,128)(2,1)} %constant.252.clone.pick_in), custom_call_target="tpu_custom_call" | custom-call | flops 1000000000 | bytes 4325404 | tf_op jit(solution)/shard_map/pack_fine/pallas_call | solution.py:471
  5.3 8.1 %all-to-all-start = ((f32[16,72,128]{2,1,0:T(8,128)}), f32[16,72,128]{2,1,0:T(8,128)S(1)}, u32[]{:S(2)}, u32[]{:S(2)}) async-start(f32[16,72,128]{2,1,0:T(8,128)} %get-tuple-element.513), calls=%async_computation | async-start | bytes 1179648 | tf_op jit(solution)/shard_map/all_to_all | solution.py:490
  13.5 5.9 %pack_coarse.1 = (f32[2688,128]{1,0:T(8,128)S(1)}, f32[6,48,128]{2,1,0:T(8,128)S(1)}, f32[6,48,128]{2,1,0:T(8,128)S(1)}) custom-call(f32[21]{0:T(128)} %rate.5, s32[1,6]{1,0:T(1,128)} %source_in.3, f32[1,21,32,1024]{3,2,1,0:T(8,128)} %coarse_in.1, f32[288,512]{1,0:T(8,128)} %get-tuple-element.514.weighted_in, bf16[1024,256]{1,0:T(8,128)(2,1)} %constant.254.clone.pick_in, ...), custom_call_target="tpu_custom_call" | custom-call | flops 1000000000 | bytes 5800044 | tf_op jit(solution)/shard_map/pack_coarse/pallas_call | solution.py:471
  19.4 6.3 %all-to-all-done.own = f32[16,72,128]{2,1,0:T(8,128)S(1)} async-done(((f32[16,72,128]{2,1,0:T(8,128)}), f32[16,72,128]{2,1,0:T(8,128)S(1)}, u32[]{:S(2)}, u32[]{:S(2)}) %all-to-all-start) | async-done | bytes 589856 | tf_op jit(solution)/shard_map/all_to_all | solution.py:490
  25.7 1.3 %collective-permute-start.3 = (f32[16,72,128]{2,1,0:T(8,128)S(1)}, f32[16,72,128]{2,1,0:T(8,128)S(1)}, u32[]{:S(2)}, u32[]{:S(2)}) collective-permute-start(f32[16,72,128]{2,1,0:T(8,128)S(1)} %all-to-all-done.own), channel_id=1, source_target_pairs={{16,0},{32,16},{48,32},{64,48},{80,64},{96,80},{112,96},{17,1},{33... | collective-permute-start | bytes 1769480 | tf_op jit(solution)/shard_map/ppermute | solution.py:486
  27.0 3.1 %collective-permute-start.2 = (f32[16,72,128]{2,1,0:T(8,128)S(1)}, f32[16,72,128]{2,1,0:T(8,128)S(1)}, u32[]{:S(2)}, u32[]{:S(2)}) collective-permute-start(f32[16,72,128]{2,1,0:T(8,128)S(1)} %all-to-all-done.own), channel_id=1, source_target_pairs={{0,16},{16,32},{32,48},{48,64},{64,80},{80,96},{96,112},{1,17},{17... | collective-permute-start | bytes 1769480 | tf_op jit(solution)/shard_map/ppermute | solution.py:486
  30.1 1.9 %choose.1 = (f32[16,72,128]{2,1,0:T(8,128)S(1)}, s32[17]{0:T(128)S(1)}) custom-call(s32[16,8]{1,0:T(8,128)S(1)} %bitcast.20, f32[2688,128]{1,0:T(8,128)S(1)} %get-tuple-element.515.packed), custom_call_target="tpu_custom_call" | custom-call | flops 1000000000 | bytes 1966660 | tf_op jit(solution)/shard_map/choose/pallas_call | solution.py:471
  32.0 0.0 copy-start.3
  32.0 16.7 %all_to_all.15.got = f32[16,72,128]{2,1,0:T(8,128)S(1)} all-to-all(f32[16,72,128]{2,1,0:T(8,128)S(1)} %get-tuple-element.517), channel_id=1, replica_groups=mesh['sfc'=8,'node'=16] {'node'}, dimensions={0} | all-to-all | bytes 1179648 | tf_op jit(solution)/shard_map/all_to_all | solution.py:490
  48.7 0.0 collective-permute-done.3.after
  48.7 0.0 collective-permute-done.2.before
  48.7 0.0 copy-done.3
  48.7 3.2 %relay.1 = (f32[16,120,128]{2,1,0:T(8,128)}, s32[23]{0:T(128)S(1)}) custom-call(s32[16,8]{1,0:T(8,128)S(1)} %bitcast.21, s32[17]{0:T(128)S(1)} %get-tuple-element.516.chosen, f32[21]{0:T(128)S(1)} %copy-done.3, f32[16,72,128]{2,1,0:T(8,128)S(1)} %collective-permute-done.2.before, f32[16,72,128]{2,1,0:T(8,128)S(1)} %all-to-all-done.own, ...), custom_call_target="tpu_custom_call" | custom-call | flops 1000000000 | bytes 3343092 | tf_op jit(solution)/shard_map/relay/pallas_call | solution.py:471
  52.0 4.3 %all-to-all-start.2 = ((f32[16,120,128]{2,1,0:T(8,128)}), f32[16,120,128]{2,1,0:T(8,128)}, u32[]{:S(2)}, u32[]{:S(2)}) async-start(f32[16,120,128]{2,1,0:T(8,128)} %get-tuple-element.519.later), calls=%async_computation.2 | async-start | bytes 1966080 | tf_op jit(solution)/shard_map/all_to_all | solution.py:490
  56.3 0.1 copy.16
  56.4 0.0 copy-start.1
  56.4 0.0 copy-start.2
  56.5 1.8 %conditional.1 = (f32[6,48,128]{2,1,0:T(8,128)}, f32[2304,128]{1,0:T(8,128)}) conditional(s32[]{:T(128)} %bitcast.10, (f32[2688,128]{1,0:T(8,128)S(1)}, f32[6,48,128]{2,1,0:T(8,128)S(1)}) %tuple.69, (f32[2688,128]{1,0:T(8,128)S(1)}, s32[16,8]{0,1:T(8,128)S(1)}, f32[6,48,128]{2,1,0:T(8,128)S(1)}, f32[6,48,128]{2,1,0:T(8,128)S(1)}) %tuple.101), branch_computations={%region_0.0_spmd, %region_1.6_spmd} | conditional | flops 221269 | bytes 12977736 | solution.py:581
  56.5 0.7 copy.39
  57.1 1.1 %slice.10 = f32[2304,128]{1,0:T(8,128)} slice(f32[2688,128]{1,0:T(8,128)S(1)} %get-tuple-element.478), slice={[0:2304], [0:128]} | slice | bytes 2359296 | tf_op jit(solution)/shard_map/cond/branch_0_fun/slice | solution.py:584
  58.2 0.0 copy-done.1
  58.2 0.0 copy-done.2
  58.2 0.0 copy-start
  58.2 1.8 %copy-done = f32[1,21,32,1024]{3,2,1,0:T(8,128)S(1)} copy-done((f32[1,21,32,1024]{3,2,1,0:T(8,128)S(1)}, f32[1,21,32,1024]{3,2,1,0:T(8,128)}, u32[]{:S(2)}) %copy-start) | copy-done | bytes 2752536
  60.0 6.6 %inner.1 = f32[1,22,32,1024]{3,2,1,0:T(8,128)S(1)} custom-call(f32[21]{0:T(128)S(1)} %copy-done.3, f32[1,21,32,1024]{3,2,1,0:T(8,128)S(1)} %copy-done, f32[1,32,1024]{2,1,0:T(8,128)S(1)} %copy-done.1, f32[21,21]{1,0:T(8,128)S(1)} %copy-done.2, f32[16,120,128]{2,1,0:T(8,128)} %get-tuple-element.519.later), custom_call_target="tpu_custom_call" | custom-call | flops 1000000000 | bytes 6752056 | tf_op jit(solution)/shard_map/inner/pallas_call | solution.py:471
  66.6 6.7 %all-to-all-done.2.got = f32[16,120,128]{2,1,0:T(8,128)} async-done(((f32[16,120,128]{2,1,0:T(8,128)}), f32[16,120,128]{2,1,0:T(8,128)}, u32[]{:S(2)}, u32[]{:S(2)}) %all-to-all-start.2) | async-done | bytes 983072 | tf_op jit(solution)/shard_map/all_to_all | solution.py:490
  73.3 4.7 %outer.1 = (f32[1,21,32,1024]{3,2,1,0:T(8,128)}, f32[1,21,48,256]{3,2,1,0:T(8,128)}) custom-call(f32[21]{0:T(128)S(1)} %copy-done.3, s32[23]{0:T(128)S(1)} %get-tuple-element.518.plan, f32[16,120,128]{2,1,0:T(8,128)} %all-to-all-done.2.got, f32[1,22,32,1024]{3,2,1,0:T(8,128)S(1)} %inner.1, f32[6,48,128]{2,1,0:T(8,128)} %get-tuple-element.522.ghost_in, ...), custom_call_target="tpu_custom_call" | custom-call | flops 1000000000 | bytes 8978608 | tf_op jit(solution)/shard_map/outer/pallas_call | solution.py:471
  (1 shorter events, 0.0 us)
Async XLA Ops:
  5.3 20.4 %all-to-all-start = ((f32[16,72,128]{2,1,0:T(8,128)}), f32[16,72,128]{2,1,0:T(8,128)S(1)}, u32[]{:S(2)}, u32[]{:S(2)}) async-start(f32[16,72,128]{2,1,0:T(8,128)} %get-tuple-element.513), calls=%async_computation | async-start | bytes 1179648 | tf_op jit(solution)/shard_map/all_to_all | solution.py:490
  25.7 23.0 %collective-permute-start.3 = (f32[16,72,128]{2,1,0:T(8,128)S(1)}, f32[16,72,128]{2,1,0:T(8,128)S(1)}, u32[]{:S(2)}, u32[]{:S(2)}) collective-permute-start(f32[16,72,128]{2,1,0:T(8,128)S(1)} %all-to-all-done.own), channel_id=1, source_target_pairs={{16,0},{32,16},{48,32},{64,48},{80,64},{96,80},{112,96},{17,1},{33... | collective-permute-start | bytes 1769480 | tf_op jit(solution)/shard_map/ppermute | solution.py:486
  27.0 21.7 %collective-permute-start.2 = (f32[16,72,128]{2,1,0:T(8,128)S(1)}, f32[16,72,128]{2,1,0:T(8,128)S(1)}, u32[]{:S(2)}, u32[]{:S(2)}) collective-permute-start(f32[16,72,128]{2,1,0:T(8,128)S(1)} %all-to-all-done.own), channel_id=1, source_target_pairs={{0,16},{16,32},{32,48},{48,64},{64,80},{80,96},{96,112},{1,17},{17... | collective-permute-start | bytes 1769480 | tf_op jit(solution)/shard_map/ppermute | solution.py:486
  32.0 16.7 %copy-start.3 = (f32[21]{0:T(128)S(1)}, f32[21]{0:T(128)}, u32[]{:S(2)}) copy-start(f32[21]{0:T(128)} %rate.5) | copy-start | bytes 256
  52.0 21.4 %all-to-all-start.2 = ((f32[16,120,128]{2,1,0:T(8,128)}), f32[16,120,128]{2,1,0:T(8,128)}, u32[]{:S(2)}, u32[]{:S(2)}) async-start(f32[16,120,128]{2,1,0:T(8,128)} %get-tuple-element.519.later), calls=%async_computation.2 | async-start | bytes 1966080 | tf_op jit(solution)/shard_map/all_to_all | solution.py:490
  56.4 1.8 %copy-start.1 = (f32[1,32,1024]{2,1,0:T(8,128)S(1)}, f32[1,32,1024]{2,1,0:T(8,128)}, u32[]{:S(2)}) copy-start(f32[1,32,1024]{2,1,0:T(8,128)} %conduct.1) | copy-start | bytes 393220
  56.4 1.8 %copy-start.2 = (f32[21,21]{1,0:T(8,128)S(1)}, f32[21,21]{1,0:T(8,128)}, u32[]{:S(2)}) copy-start(f32[21,21]{1,0:T(8,128)} %react.1) | copy-start | bytes 5296
  58.2 1.8 %copy-start = (f32[1,21,32,1024]{3,2,1,0:T(8,128)S(1)}, f32[1,21,32,1024]{3,2,1,0:T(8,128)}, u32[]{:S(2)}) copy-start(f32[1,21,32,1024]{3,2,1,0:T(8,128)} %state.1) | copy-start | bytes 8257540
